TPU v7x, 128 devices: a whole 4x4x4 slice. The times are simulated.
128 devices in a mesh: row: 8 (over y, x_lo), col: 16 (over z, x_hi, core).
Axes of the slice: x: 4 (x_hi: 2, x_lo: 2; x = x_hi * 2 + x_lo), y: 4, z: 4, core: 2. Of those that a mesh axis runs over, the one named last changes fastest.
Arguments:
- spectra: bfloat16 [16384, 1024], P(('row', 'col')), may hold values from -6 to 6
Outputs:
- coherence: float32 [2, 16384, 16384], P(None, 'row', 'col')
All inputs are finite; a program needn't handle non-finite values.
Results may differ from a plain program's by a relative error of at most 0.0003.
Values may be sent and summed in bfloat16 or wider, within the bound.
No kernel may reach another device: no remote copies, remote signals or barrier semaphores. Data moves between devices by JAX's collectives and lax.ppermute only.
A program may use at most 128 MiB of HBM per device.

v0:
```python
import jax
import jax.numpy as jnp
from jax import lax
from jax.sharding import PartitionSpec as P

TAPERS = 8
BINS = 64


def shards(spectra):
    row_block = lax.all_gather(spectra, "col", axis=0, tiled=True)
    ratio = lax.axis_size("col") // lax.axis_size("row")
    col_index = lax.axis_index("col")
    width = row_block.shape[0] // ratio
    everything = lax.all_gather(spectra, ("row", "col"), axis=0, tiled=True)
    col_block = lax.dynamic_slice_in_dim(everything, col_index * width, width, 0)
    half = TAPERS * BINS
    turned = jnp.concatenate([-col_block[:, half:], col_block[:, :half]], axis=1)
    stacked = jnp.concatenate([col_block, turned], axis=0)
    cross = lax.dot_general(
        row_block, stacked, (((1,), (1,)), ((), ())), preferred_element_type=jnp.float32
    )
    row_values = row_block.astype(jnp.float32)
    col_values = col_block.astype(jnp.float32)
    row_root = jnp.sqrt(jnp.sum(row_values * row_values, axis=1))
    col_root = jnp.sqrt(jnp.sum(col_values * col_values, axis=1))
    scale = row_root[:, None] * col_root[None, :]
    real_part = cross[:, :width] / scale
    imag_part = cross[:, width:] / scale
    return jnp.stack([real_part, imag_part], axis=0)


def solution(mesh):
    placed = (P(("row", "col"), None),)
    return jax.shard_map(
        shards, mesh=mesh, in_specs=placed, out_specs=P(None, "row", "col"), check_vma=False
    )
```

profile of v0, /device:TPU:1, one launch (start us, length us, event | category | flops | bytes accessed | tf_op | source)
XLA Modules:
  0.0 366.0 jit_solution(2247700307793745255)
XLA Ops:
  6.5 0.0 all-gather.5.cloned.1.call-start
  6.5 0.7 all-gather.5.cloned.1.call-update
  7.3 0.0 all-gather.3.cloned.1.call-start
  7.3 0.7 all-gather.3.cloned.1.call-update
  8.0 60.9 %all-gather.5.cloned.1.call-done = bf16[2048,1024]{1,0:T(8,128)(2,1)} async-done(((bf16[128,1024]{1,0:T(8,128)(2,1)}), bf16[2048,1024]{1,0:T(8,128)(2,1)}) %all-gather.5.cloned.1.call-update) | async-done | bytes 4194320 | tf_op jit(solution)/shard_map/all_gather | solution.py:11
  68.9 3.1 multiply_reduce_fusion
  72.0 233.2 %all-gather.3.cloned.1.call-done = bf16[16384,1024]{1,0:T(8,128)(2,1)} async-done(((bf16[128,1024]{1,0:T(8,128)(2,1)}), bf16[16384,1024]{1,0:T(8,128)(2,1)}) %all-gather.3.cloned.1.call-update) | async-done | bytes 33554448 | tf_op jit(solution)/shard_map/all_gather | solution.py:15
  305.2 0.0 copy-start
  305.2 2.2 multiply_reduce_fusion.1
  307.4 1.8 dynamic-slice_negate_fusion
  309.3 0.0 copy-done
  309.3 18.8 %convolution_bitcast_fusion = f32[2048,2048]{0,1:T(8,128)} fusion(bf16[2048,1024]{1,0:T(8,128)(2,1)S(1)} %copy-done, bf16[1024,512]{1,0:T(8,128)(2,1)S(1)} %get-tuple-element.8, bf16[1024,512]{1,0:T(8,128)(2,1)S(1)} %get-tuple-element.7, bf16[1024,1024]{1,0:T(8,128)(2,1)S(1)} %get-tuple-element.6), kind=kOutput, calls=%fused_computation.3 | convolution fusion | flops 8602517504 | bytes 25165824 | tf_op jit(solution)/shard_map/dot_general | solution.py:20
  328.0 7.1 %fusion = (f32[1,2048,1024]{1,2,0:T(8,128)S(1)}, f32[1,2048,1024]{1,2,0:T(8,128)S(1)}) fusion(f32[2048,2048]{0,1:T(8,128)} %convolution_bitcast_fusion, f32[1024]{0:T(1024)S(1)} %sqrt.15, f32[2048]{0:T(1024)S(1)} %sqrt.14), kind=kLoop, calls=%fused_computation.4 | loop fusion | flops 6291456 | bytes 33566720 | tf_op jit(solution)/shard_map/stack | solution.py:30
  335.2 6.0 %pad_maximum_fusion = f32[2,2048,1024]{1,2,0:T(8,128)} fusion(f32[1,2048,1024]{1,2,0:T(8,128)S(1)} %get-tuple-element.10, f32[1,2048,1024]{1,2,0:T(8,128)S(1)} %get-tuple-element.9), kind=kLoop, calls=%fused_computation | loop fusion | flops 4194304 | bytes 33554432 | tf_op jit(solution)/shard_map/stack | solution.py:30
  341.2 18.0 %copy.2 = f32[2,2048,1024]{2,1,0:T(8,128)} copy(f32[2,2048,1024]{1,2,0:T(8,128)} %pad_maximum_fusion) | data formatting | bytes 33554432 | tf_op jit(solution)/shard_map/stack | solution.py:30
  (2 shorter events, 0.0 us)
Async XLA Ops:
  6.5 62.4 %all-gather.5.cloned.1.call-start = ((), (), s32[]{:S(2)}) async-start(), calls=%async_computation.1 | async-start | bytes 4456448 | tf_op jit(solution)/shard_map/all_gather | solution.py:11
  7.3 297.9 %all-gather.3.cloned.1.call-start = ((), (), s32[]{:S(2)}) async-start(), calls=%async_computation | async-start | bytes 33816576 | tf_op jit(solution)/shard_map/all_gather | solution.py:15
  305.2 4.1 %copy-start = (bf16[2048,1024]{1,0:T(8,128)(2,1)S(1)}, bf16[2048,1024]{1,0:T(8,128)(2,1)}, u32[]{:S(2)}) copy-start(bf16[2048,1024]{1,0:T(8,128)(2,1)} %all-gather.5.cloned.1.call-done) | copy-start | bytes 12582916
Sparse Core Ops, SparseCore 0:
  9.8 59.0 all-gather.4
  70.7 234.5 all-gather.2
where the time goes:
time: 366 us
  waiting for transfers between devices  296 us (81%)
  other arithmetic  20.2 us (6%)
  matrix products  18.8 us (5%)
  local copies, waits for them, and re-layouts  18 us (5%)
  between operations  13.4 us (4%)
    all_gather x1, waiting for transfers between devices, shards(): everything = lax.all_gather(spectra, ('row', 'col'), axis=0, tiled=True)  233 us
    all_gather x1, waiting for transfers between devices, shards(): row_block = lax.all_gather(spectra, 'col', axis=0, tiled=True)  60.9 us
    dot_general x1, matrix products, shards(): lax.dot_general(row_block, stacked, (((1,), (1,)), ((), ())), preferred_e...  18.8 us
    another operation x1, local copies, waits for them, and re-layouts, shards(): return jnp.stack([real_part, imag_part], axis=0)  18 us
    another operation x2, other arithmetic, shards(): return jnp.stack([real_part, imag_part], axis=0)  13.1 us
  transfers between devices with their start and end apart: 2, of which 2 were waited for; matrix products, arithmetic and copies ran while one was open for 1% of the time, Pallas kernels for 0%

commit v1 on v0

v1 whole, which is shorter than its diff:
```python
import functools

import jax
import jax.numpy as jnp
from jax import lax
from jax.experimental import pallas as pl
from jax.experimental.pallas import tpu as pltpu
from jax.sharding import PartitionSpec as P

TAPERS = 8
BINS = 64
HALF = TAPERS * BINS
SPEC = 2 * HALF
AXES = ("row", "col")
NT = (((1,), (1,)), ((), ()))
F32, BF16 = jnp.float32, jnp.bfloat16
SHARD = 128
TILE = 256


def place(i):
    row, col = divmod(i, 16)
    return (col // 2 % 2) * 2 + row % 2, row // 2, col // 4, col % 2


def number(x, y, z, core):
    return (y * 2 + x % 2) * 16 + z * 4 + (x // 2) * 2 + core


def moves(rule):
    return [(i, number(*rule(*place(i)))) for i in range(128)]


SWAP_CORE = moves(lambda x, y, z, c: (x, y, z, 1 - c))
ACROSS_X = moves(lambda x, y, z, c: ((x + 2) % 4, y, z, c))
Y_UP = moves(lambda x, y, z, c: (x, (y + 1) % 4, z, c))
Y_DOWN = moves(lambda x, y, z, c: (x, (y + 3) % 4, z, c))
Z_RINGS = [[z * 4 + r for z in range(4)] for r in range(4)]


def to_columns(flip):
    def rule(x, y, z, c):
        low = c ^ flip
        return 2 * (x % 2) + low, (y + 2 * (z % 2) + x // 2) % 4, y, z // 2

    return moves(rule)


COLS_A, COLS_B = to_columns(0), to_columns(1)


def send(value, pairs):
    return lax.ppermute(value, AXES, pairs)


def together(*values):
    return lax.optimization_barrier(values)


def pair(a, b):
    return jnp.concatenate([a, b], axis=0)


def spots():
    row, col = lax.axis_index("row"), lax.axis_index("col")
    return row % 2, col // 2 % 2, row // 2, col // 4, col % 2


def kernel(pos, a0, a1, a2, a3, c_own, c_up, c_down, c_far0, c_far1, out, a_all, b, turned, col_inv, sems):
    step = pl.program_id(0)
    low, q = pos[1], pos[2]

    def a_copy(j):
        src = (a0, a1, a2, a3)[j]
        return pltpu.make_async_copy(src, a_all.at[pl.ds(j * 512, 512)], sems.at[j])

    def b_copies():
        copies = []
        for n, (src, turn) in enumerate(((c_own, 0), (c_up, 3), (c_down, 1), (c_far0, 2), (c_far1, 2))):
            base = lax.rem(q + turn, 4) * (2 * SHARD)
            if n < 3:
                for m in range(2):
                    at = pl.multiple_of(base + (low if m == 0 else 1 - low) * SHARD, SHARD)
                    copies.append((src.at[pl.ds(m * SHARD, SHARD)], at))
            else:
                at = pl.multiple_of(base + (low if n == 3 else 1 - low) * SHARD, SHARD)
                copies.append((src, at))
        return [
            pltpu.make_async_copy(s, b.at[pl.ds(at, SHARD)], sems.at[4 + m])
            for m, (s, at) in enumerate(copies)
        ]

    @pl.when(step == 0)
    def _():
        for copy in b_copies():
            copy.start()
        for j in range(4):
            a_copy(j).start()
        for copy in b_copies():
            copy.wait()
        values = b[...]
        turned[:, :HALF] = -values[:, HALF:]
        turned[:, HALF:] = values[:, :HALF]
        squares = values.astype(F32)
        squares = squares * squares
        high = squares.astype(BF16)
        rest = (squares - high.astype(F32)).astype(BF16)
        ones = jnp.ones((8, SPEC), BF16)
        power = lax.dot_general(ones, high, NT, preferred_element_type=F32)
        power += lax.dot_general(ones, rest, NT, preferred_element_type=F32)
        col_inv[...] = 1.0 / jnp.sqrt(power)

    for j in range(4):
        @pl.when(step == 2 * j)
        def _():
            a_copy(j).wait()

    a = a_all[pl.ds(pl.multiple_of(step * TILE, TILE), TILE), :]
    values = a.astype(F32)
    row_inv = 1.0 / jnp.sqrt(jnp.sum(values * values, axis=1, keepdims=True))
    scale = col_inv[0:1, :]
    real = lax.dot_general(a, b[...], NT, preferred_element_type=F32)
    out[0, :, 0] = (real * row_inv * scale).reshape(2, SHARD, 1024)
    imag = lax.dot_general(a, turned[...], NT, preferred_element_type=F32)
    out[1, :, 0] = (imag * row_inv * scale).reshape(2, SHARD, 1024)


def coherence(pos, rows, cols):
    def place_out(step, pos):
        j = step // 2
        spot = pos[0] ^ jnp.where(j % 2 == 1, 1, 0) ^ jnp.where(j // 2 == 1, 2, 0)
        return 0, step % 2, spot, 0, 0

    anywhere = pl.BlockSpec(memory_space=pl.ANY)
    out = pl.pallas_call(
        kernel,
        grid_spec=pltpu.PrefetchScalarGridSpec(
            num_scalar_prefetch=1,
            grid=(8,),
            in_specs=[anywhere] * 9,
            out_specs=pl.BlockSpec((2, 2, 1, SHARD, 1024), place_out),
            scratch_shapes=[
                pltpu.VMEM((2048, SPEC), BF16),
                pltpu.VMEM((1024, SPEC), BF16),
                pltpu.VMEM((1024, SPEC), BF16),
                pltpu.VMEM((8, 1024), F32),
                pltpu.SemaphoreType.DMA((12,)),
            ],
        ),
        out_shape=jax.ShapeDtypeStruct((2, 4, 4, SHARD, 1024), F32),
        compiler_params=pltpu.CompilerParams(vmem_limit_bytes=40 * 2**20),
        cost_estimate=pl.CostEstimate(flops=8 * 2**30, bytes_accessed=22 * 2**20, transcendentals=4096),
        name="coherence",
    )(pos, *rows, *cols)
    return out.reshape(2, 2048, 1024)


def shards(x):
    low, high, y, z, core = spots()
    pos = jnp.stack([high * 2 + core, low, (y + 4 - z) % 4]).astype(jnp.int32)
    own = lax.all_gather(x, "col", axis=0, tiled=True, axis_index_groups=Z_RINGS)
    c0, c1, across = send(x, COLS_A), send(x, COLS_B), send(x, ACROSS_X)
    other = lax.all_gather(across, "col", axis=0, tiled=True, axis_index_groups=Z_RINGS)
    c_own = pair(c0, c1)
    c_up, c_down = send(c_own, Y_UP), send(c_own, Y_DOWN)
    c_up, c_down, own = together(c_up, c_down, own)
    far0, far1 = send(c_up[:SHARD], Y_UP), send(c_down[SHARD:], Y_DOWN)
    own_swapped = send(own, SWAP_CORE)
    other_swapped = send(other, SWAP_CORE)
    rows = (own, own_swapped, other, other_swapped)
    return coherence(pos, rows, (c_own, c_up, c_down, far0, far1))


def solution(mesh):
    return jax.shard_map(
        shards, mesh=mesh, in_specs=(P(AXES, None),), out_specs=P(None, "row", "col"), check_vma=False
    )
```

time: 366 us -> 109 us (0.30)
  waiting for transfers between devices: 296 us -> 60.7 us
  other arithmetic: 20.2 us -> 0.08 us
  matrix products: 18.8 us -> 0 us
  starting transfers between devices: 0.04 us -> 16.1 us
  Pallas kernels: 0 us -> 14.6 us
  local copies, waits for them, and re-layouts: 18 us -> 3.93 us
    all_gather x2, waiting for transfers between devices: 294 us -> 13.5 us  [the longest x1 13.5 us: shards(): lax.all_gather(across, 'col', axis=0, tiled=True, axis_index_groups=Z_RINGS)]
    ppermute x0 -> x9, waiting for transfers between devices: none -> 46.5 us  [send(): return lax.ppermute(value, AXES, pairs)]
    dot_general x1 -> x0, matrix products: 18.8 us -> none  [shards(): lax.dot_general(row_block, stacked, (((1,), (1,)), ((), ())), preferred_e...]
    another operation x1 -> x0, local copies, waits for them, and re-layouts: 18 us -> none  [shards(): return jnp.stack([real_part, imag_part], axis=0)]
    ppermute x0 -> x9, starting transfers between devices: none -> 16.1 us  [send(): return lax.ppermute(value, AXES, pairs)]
    pallas_call x0 -> x1, Pallas kernels: none -> 14.6 us  [coherence(): pl.pallas_call(kernel, grid_spec=pltpu.PrefetchScalarGridSpec(num_scalar_...]
    another operation x2 -> x1, other arithmetic: 13.1 us -> 0.08 us  [shards(): pos = jnp.stack([high * 2 + core, low, (y + 4 - z) % 4]).astype(jnp.int32)]
    reduce_sum x2 -> x0, other arithmetic: 5.29 us -> none  [the longest x1 3.07 us: shards(): row_root = jnp.sqrt(jnp.sum(row_values * row_values, axis=1))]
  transfers between devices with their start and end apart: 2 -> 11, of which waited for: 2 -> 8; matrix products, arithmetic and copies ran while one was open for 1% -> 1% of each run, Pallas kernels for 0% -> 0%
where the time goes in v1:
time: 109 us
  waiting for transfers between devices  60.7 us (56%)
  starting transfers between devices  16.1 us (15%)
  Pallas kernels  14.6 us (13%)
  between operations  13.5 us (12%)
  local copies, waits for them, and re-layouts  3.93 us (4%)
    ppermute x9, waiting for transfers between devices, send(): return lax.ppermute(value, AXES, pairs)  46.5 us
    ppermute x9, starting transfers between devices, send(): return lax.ppermute(value, AXES, pairs)  16.1 us
    pallas_call x1, Pallas kernels, coherence(): pl.pallas_call(kernel, grid_spec=pltpu.PrefetchScalarGridSpec(num_scalar_...  14.6 us
    all_gather x1, waiting for transfers between devices, shards(): lax.all_gather(across, 'col', axis=0, tiled=True, axis_index_groups=Z_RINGS)  13.5 us
    unnamed x7, local copies, waits for them, and re-layouts  3.17 us
  transfers between devices with their start and end apart: 11, of which 8 were waited for; matrix products, arithmetic and copies ran while one was open for 1% of the time, Pallas kernels for 0%

profile of v1, /device:TPU:1, one launch (start us, length us, event | category | flops | bytes accessed | tf_op | source)
XLA Modules:
  0.0 108.9 jit_solution(4156773172698681046)
XLA Ops:
  6.5 0.0 all-gather.3.cloned.1.call-start
  6.5 0.7 all-gather.3.cloned.1.call-update
  7.3 0.0 all-gather.5.cloned.1.call-start
  7.3 3.7 %collective-permute-start.5 = (bf16[128,1024]{1,0:T(8,128)(2,1)}, bf16[128,1024]{1,0:T(8,128)(2,1)S(1)}, u32[]{:S(2)}, u32[]{:S(2)}) collective-permute-start(bf16[128,1024]{1,0:T(8,128)(2,1)} %param.1), channel_id=1, source_target_pairs={{0,2},{1,3},{2,0},{3,1},{4,6},{5,7},{6,4},{7,5},{8,10},{9,11},{10,... | collective-permute-start | bytes 786440 | tf_op jit(solution)/shard_map/ppermute | solution.py:53
  11.0 5.8 %collective-permute-done.5 = bf16[128,1024]{1,0:T(8,128)(2,1)S(1)} collective-permute-done((bf16[128,1024]{1,0:T(8,128)(2,1)}, bf16[128,1024]{1,0:T(8,128)(2,1)S(1)}, u32[]{:S(2)}, u32[]{:S(2)}) %collective-permute-start.5) | collective-permute-done | bytes 262176 | tf_op jit(solution)/shard_map/ppermute | solution.py:53
  16.7 0.0 copy-start.2
  16.7 0.7 copy-done.2
  17.4 0.0 all-gather.5.cloned.1.call-update
  17.4 4.9 %collective-permute-start = (bf16[128,1024]{1,0:T(8,128)(2,1)}, bf16[128,1024]{1,0:T(8,128)(2,1)S(1)}, u32[]{:S(2)}, u32[]{:S(2)}) collective-permute-start(bf16[128,1024]{1,0:T(8,128)(2,1)} %param.1), channel_id=1, source_target_pairs={{0,0},{1,16},{2,32},{3,48},{4,64},{5,80},{6,96},{7,112},{8,1},{9,1... | collective-permute-start | bytes 786440 | tf_op jit(solution)/shard_map/ppermute | solution.py:53
  22.4 1.9 %collective-permute-start.1 = (bf16[128,1024]{1,0:T(8,128)(2,1)}, bf16[128,1024]{1,0:T(8,128)(2,1)S(1)}, u32[]{:S(2)}, u32[]{:S(2)}) collective-permute-start(bf16[128,1024]{1,0:T(8,128)(2,1)} %param.1), channel_id=1, source_target_pairs={{0,16},{1,0},{2,48},{3,32},{4,80},{5,64},{6,112},{7,96},{8,17},{9,... | collective-permute-start | bytes 786440 | tf_op jit(solution)/shard_map/ppermute | solution.py:53
  24.3 17.8 %collective-permute-done = bf16[128,1024]{1,0:T(8,128)(2,1)S(1)} collective-permute-done((bf16[128,1024]{1,0:T(8,128)(2,1)}, bf16[128,1024]{1,0:T(8,128)(2,1)S(1)}, u32[]{:S(2)}, u32[]{:S(2)}) %collective-permute-start) | collective-permute-done | bytes 262176 | tf_op jit(solution)/shard_map/ppermute | solution.py:53
  42.1 1.5 %collective-permute-done.1 = bf16[128,1024]{1,0:T(8,128)(2,1)S(1)} collective-permute-done((bf16[128,1024]{1,0:T(8,128)(2,1)}, bf16[128,1024]{1,0:T(8,128)(2,1)S(1)}, u32[]{:S(2)}, u32[]{:S(2)}) %collective-permute-start.1) | collective-permute-done | bytes 262176 | tf_op jit(solution)/shard_map/ppermute | solution.py:53
  43.7 0.1 collective-permute-start.3
  43.8 1.5 %collective-permute-start.2 = (bf16[256,1024]{1,0:T(8,128)(2,1)S(1)}, bf16[256,1024]{1,0:T(8,128)(2,1)S(1)}, u32[]{:S(2)}, u32[]{:S(2)}) collective-permute-start(bf16[256,1024]{1,0:T(8,128)(2,1)S(1)} %constant_dynamic-update-slice_fusion.c_own), channel_id=1, source_target_pairs={{0,32},{1,33},{2,34},{3,35},{4,36},{5,37},{6,38},{7,39},{8,40},{9,... | collective-permute-start | bytes 1572872 | tf_op jit(solution)/shard_map/ppermute | solution.py:53
  45.2 9.2 %collective-permute-done.3.c_down = bf16[256,1024]{1,0:T(8,128)(2,1)S(1)} collective-permute-done((bf16[256,1024]{1,0:T(8,128)(2,1)S(1)}, bf16[256,1024]{1,0:T(8,128)(2,1)S(1)}, u32[]{:S(2)}, u32[]{:S(2)}) %collective-permute-start.3) | collective-permute-done | bytes 524320 | tf_op jit(solution)/shard_map/ppermute | solution.py:53
  54.4 3.4 %collective-permute-done.2.c_up = bf16[256,1024]{1,0:T(8,128)(2,1)S(1)} collective-permute-done((bf16[256,1024]{1,0:T(8,128)(2,1)S(1)}, bf16[256,1024]{1,0:T(8,128)(2,1)S(1)}, u32[]{:S(2)}, u32[]{:S(2)}) %collective-permute-start.2) | collective-permute-done | bytes 524320 | tf_op jit(solution)/shard_map/ppermute | solution.py:53
  57.8 0.0 all-gather.3.cloned.1.call-done.a0
  57.8 0.0 collective-permute-start.4
  57.8 13.5 %all-gather.5.cloned.1.call-done.a2 = bf16[512,1024]{1,0:T(8,128)(2,1)} async-done(((bf16[128,1024]{1,0:T(8,128)(2,1)}), bf16[512,1024]{1,0:T(8,128)(2,1)}) %all-gather.5.cloned.1.call-update) | async-done | bytes 1048592 | tf_op jit(solution)/shard_map/all_gather | solution.py:163
  71.4 1.6 %collective-permute-start.6 = (bf16[512,1024]{1,0:T(8,128)(2,1)}, bf16[512,1024]{1,0:T(8,128)(2,1)}, u32[]{:S(2)}, u32[]{:S(2)}) collective-permute-start(bf16[512,1024]{1,0:T(8,128)(2,1)} %all-gather.5.cloned.1.call-done.a2), channel_id=1, source_target_pairs={{0,1},{1,0},{2,3},{3,2},{4,5},{5,4},{6,7},{7,6},{8,9},{9,8},{10,11... | collective-permute-start | bytes 3145736 | tf_op jit(solution)/shard_map/ppermute | solution.py:53
  73.0 0.7 slice.7
  73.7 2.5 %collective-permute-start.8 = (bf16[128,1024]{1,0:T(8,128)(2,1)}, bf16[128,1024]{1,0:T(8,128)(2,1)S(1)}, u32[]{:S(2)}, u32[]{:S(2)}) collective-permute-start(bf16[128,1024]{1,0:T(8,128)(2,1)} %slice.7), channel_id=1, source_target_pairs={{0,96},{1,97},{2,98},{3,99},{4,100},{5,101},{6,102},{7,103},{8,104... | collective-permute-start | bytes 786440 | tf_op jit(solution)/shard_map/ppermute | solution.py:53
  76.2 0.0 collective-permute-start.7
  76.2 0.1 pad_add_fusion.pos
  76.2 6.0 %collective-permute-done.8.c_far1 = bf16[128,1024]{1,0:T(8,128)(2,1)S(1)} collective-permute-done((bf16[128,1024]{1,0:T(8,128)(2,1)}, bf16[128,1024]{1,0:T(8,128)(2,1)S(1)}, u32[]{:S(2)}, u32[]{:S(2)}) %collective-permute-start.8) | collective-permute-done | bytes 262176 | tf_op jit(solution)/shard_map/ppermute | solution.py:53
  82.2 2.8 %collective-permute-done.7.c_far0 = bf16[128,1024]{1,0:T(8,128)(2,1)S(1)} collective-permute-done((bf16[128,1024]{1,0:T(8,128)(2,1)S(1)}, bf16[128,1024]{1,0:T(8,128)(2,1)S(1)}, u32[]{:S(2)}, u32[]{:S(2)}) %collective-permute-start.7) | collective-permute-done | bytes 262176 | tf_op jit(solution)/shard_map/ppermute | solution.py:53
  85.0 0.0 collective-permute-done.4.a1
  85.0 0.0 collective-permute-done.6.a3
  85.0 0.0 copy-start
  85.0 1.2 %copy-done = bf16[512,1024]{1,0:T(8,128)(2,1)S(1)} copy-done((bf16[512,1024]{1,0:T(8,128)(2,1)S(1)}, bf16[512,1024]{1,0:T(8,128)(2,1)}, u32[]{:S(2)}) %copy-start) | copy-done | bytes 1048600
  86.2 0.0 copy-start.1
  86.2 1.2 %copy-done.1 = bf16[512,1024]{1,0:T(8,128)(2,1)S(1)} copy-done((bf16[512,1024]{1,0:T(8,128)(2,1)S(1)}, bf16[512,1024]{1,0:T(8,128)(2,1)}, u32[]{:S(2)}) %copy-start.1) | copy-done | bytes 1048600
  87.5 14.6 %coherence.1 = f32[2,4,4,128,1024]{4,3,2,1,0:T(8,128)} custom-call(s32[3]{0:T(128)S(1)} %pad_add_fusion.pos, bf16[512,1024]{1,0:T(8,128)(2,1)S(1)} %copy-done, bf16[512,1024]{1,0:T(8,128)(2,1)S(1)} %collective-permute-done.4.a1, bf16[512,1024]{1,0:T(8,128)(2,1)S(1)} %copy-done.1, bf16[512,1024]{1,0:T(8,128)(2,1)} %collective-permute-done.6.a3, ...), custom_call_target="tpu_custom_call" | custom-call | flops 8589934592 | bytes 23068672 | tf_op jit(solution)/shard_map/coherence/pallas_call | solution.py:135
  (3 shorter events, 0.1 us)
Async XLA Ops:
  6.5 51.3 %all-gather.3.cloned.1.call-start = ((), (), s32[]{:S(2)}) async-start(), calls=%async_computation | async-start | bytes 1310720 | tf_op jit(solution)/shard_map/all_gather | solution.py:161
  7.3 64.1 %all-gather.5.cloned.1.call-start = ((), (), s32[]{:S(2)}) async-start(), calls=%async_computation.1 | async-start | bytes 1310720 | tf_op jit(solution)/shard_map/all_gather | solution.py:163
  7.3 9.4 %collective-permute-start.5 = (bf16[128,1024]{1,0:T(8,128)(2,1)}, bf16[128,1024]{1,0:T(8,128)(2,1)S(1)}, u32[]{:S(2)}, u32[]{:S(2)}) collective-permute-start(bf16[128,1024]{1,0:T(8,128)(2,1)} %param.1), channel_id=1, source_target_pairs={{0,2},{1,3},{2,0},{3,1},{4,6},{5,7},{6,4},{7,5},{8,10},{9,11},{10,... | collective-permute-start | bytes 786440 | tf_op jit(solution)/shard_map/ppermute | solution.py:53
  16.7 0.7 copy-start.2
  17.4 24.7 %collective-permute-start = (bf16[128,1024]{1,0:T(8,128)(2,1)}, bf16[128,1024]{1,0:T(8,128)(2,1)S(1)}, u32[]{:S(2)}, u32[]{:S(2)}) collective-permute-start(bf16[128,1024]{1,0:T(8,128)(2,1)} %param.1), channel_id=1, source_target_pairs={{0,0},{1,16},{2,32},{3,48},{4,64},{5,80},{6,96},{7,112},{8,1},{9,1... | collective-permute-start | bytes 786440 | tf_op jit(solution)/shard_map/ppermute | solution.py:53
  22.4 21.3 %collective-permute-start.1 = (bf16[128,1024]{1,0:T(8,128)(2,1)}, bf16[128,1024]{1,0:T(8,128)(2,1)S(1)}, u32[]{:S(2)}, u32[]{:S(2)}) collective-permute-start(bf16[128,1024]{1,0:T(8,128)(2,1)} %param.1), channel_id=1, source_target_pairs={{0,16},{1,0},{2,48},{3,32},{4,80},{5,64},{6,112},{7,96},{8,17},{9,... | collective-permute-start | bytes 786440 | tf_op jit(solution)/shard_map/ppermute | solution.py:53
  43.7 10.8 %collective-permute-start.3 = (bf16[256,1024]{1,0:T(8,128)(2,1)S(1)}, bf16[256,1024]{1,0:T(8,128)(2,1)S(1)}, u32[]{:S(2)}, u32[]{:S(2)}) collective-permute-start(bf16[256,1024]{1,0:T(8,128)(2,1)S(1)} %constant_dynamic-update-slice_fusion.c_own), channel_id=1, source_target_pairs={{0,96},{1,97},{2,98},{3,99},{4,100},{5,101},{6,102},{7,103},{8,104... | collective-permute-start | bytes 1572872 | tf_op jit(solution)/shard_map/ppermute | solution.py:53
  43.8 14.1 %collective-permute-start.2 = (bf16[256,1024]{1,0:T(8,128)(2,1)S(1)}, bf16[256,1024]{1,0:T(8,128)(2,1)S(1)}, u32[]{:S(2)}, u32[]{:S(2)}) collective-permute-start(bf16[256,1024]{1,0:T(8,128)(2,1)S(1)} %constant_dynamic-update-slice_fusion.c_own), channel_id=1, source_target_pairs={{0,32},{1,33},{2,34},{3,35},{4,36},{5,37},{6,38},{7,39},{8,40},{9,... | collective-permute-start | bytes 1572872 | tf_op jit(solution)/shard_map/ppermute | solution.py:53
  57.8 27.2 %collective-permute-start.4 = (bf16[512,1024]{1,0:T(8,128)(2,1)}, bf16[512,1024]{1,0:T(8,128)(2,1)S(1)}, u32[]{:S(2)}, u32[]{:S(2)}) collective-permute-start(bf16[512,1024]{1,0:T(8,128)(2,1)} %all-gather.3.cloned.1.call-done.a0), channel_id=1, source_target_pairs={{0,1},{1,0},{2,3},{3,2},{4,5},{5,4},{6,7},{7,6},{8,9},{9,8},{10,11... | collective-permute-start | bytes 3145736 | tf_op jit(solution)/shard_map/ppermute | solution.py:53
  71.4 13.6 %collective-permute-start.6 = (bf16[512,1024]{1,0:T(8,128)(2,1)}, bf16[512,1024]{1,0:T(8,128)(2,1)}, u32[]{:S(2)}, u32[]{:S(2)}) collective-permute-start(bf16[512,1024]{1,0:T(8,128)(2,1)} %all-gather.5.cloned.1.call-done.a2), channel_id=1, source_target_pairs={{0,1},{1,0},{2,3},{3,2},{4,5},{5,4},{6,7},{7,6},{8,9},{9,8},{10,11... | collective-permute-start | bytes 3145736 | tf_op jit(solution)/shard_map/ppermute | solution.py:53
  73.7 8.5 %collective-permute-start.8 = (bf16[128,1024]{1,0:T(8,128)(2,1)}, bf16[128,1024]{1,0:T(8,128)(2,1)S(1)}, u32[]{:S(2)}, u32[]{:S(2)}) collective-permute-start(bf16[128,1024]{1,0:T(8,128)(2,1)} %slice.7), channel_id=1, source_target_pairs={{0,96},{1,97},{2,98},{3,99},{4,100},{5,101},{6,102},{7,103},{8,104... | collective-permute-start | bytes 786440 | tf_op jit(solution)/shard_map/ppermute | solution.py:53
  76.2 8.8 %collective-permute-start.7 = (bf16[128,1024]{1,0:T(8,128)(2,1)S(1)}, bf16[128,1024]{1,0:T(8,128)(2,1)S(1)}, u32[]{:S(2)}, u32[]{:S(2)}) collective-permute-start(bf16[128,1024]{1,0:T(8,128)(2,1)S(1)} %slice.6), channel_id=1, source_target_pairs={{0,32},{1,33},{2,34},{3,35},{4,36},{5,37},{6,38},{7,39},{8,40},{9,... | collective-permute-start | bytes 786440 | tf_op jit(solution)/shard_map/ppermute | solution.py:53
  85.0 1.2 %copy-start = (bf16[512,1024]{1,0:T(8,128)(2,1)S(1)}, bf16[512,1024]{1,0:T(8,128)(2,1)}, u32[]{:S(2)}) copy-start(bf16[512,1024]{1,0:T(8,128)(2,1)} %all-gather.3.cloned.1.call-done.a0) | copy-start | bytes 3145732
  86.2 1.2 %copy-start.1 = (bf16[512,1024]{1,0:T(8,128)(2,1)S(1)}, bf16[512,1024]{1,0:T(8,128)(2,1)}, u32[]{:S(2)}) copy-start(bf16[512,1024]{1,0:T(8,128)(2,1)} %all-gather.5.cloned.1.call-done.a2) | copy-start | bytes 3145732
Sparse Core Ops, SparseCore 0:
  9.0 35.6 all-gather.2
  46.4 24.9 all-gather.4

commit v2 on v0

v2 whole, which is shorter than its diff:
```python
import jax
import jax.numpy as jnp
from jax import lax
from jax.experimental import pallas as pl
from jax.experimental.pallas import tpu as pltpu
from jax.sharding import PartitionSpec as P

TAPERS = 8
BINS = 64
HALF = TAPERS * BINS
SPEC = 2 * HALF
AXES = ("row", "col")
NT = (((1,), (1,)), ((), ()))
F32, BF16 = jnp.float32, jnp.bfloat16
SHARD = 128
COLS = 8 * SHARD
WIDE = COLS // 2
OUT = (2, 4, 2, 2, SHARD, COLS)
TILE = 2 * SHARD


def place(i):
    row, col = divmod(i, 16)
    return (col // 2 % 2) * 2 + row % 2, row // 2, col // 4, col % 2


def number(x, y, z, core):
    return (y * 2 + x % 2) * 16 + z * 4 + (x // 2) * 2 + core


def moves(rule):
    return [(i, number(*rule(*place(i)))) for i in range(128)]


SWAP_CORE = moves(lambda x, y, z, c: (x, y, z, 1 - c))
ACROSS_X = moves(lambda x, y, z, c: ((x + 2) % 4, y, z, c))
Y_UP = moves(lambda x, y, z, c: (x, (y + 1) % 4, z, c))
Y_DOWN = moves(lambda x, y, z, c: (x, (y + 3) % 4, z, c))
Z_UP = moves(lambda x, y, z, c: (x, y, (z + 1) % 4, c))
Z_DOWN = moves(lambda x, y, z, c: (x, y, (z + 3) % 4, c))
Z_SPLIT = moves(lambda x, y, z, c: (x, y, (z + 1 + 2 * c) % 4, c))


def to_columns(flip):
    def rule(x, y, z, c):
        return 2 * (x % 2) + (x // 2 ^ flip), (y + z + 2 * c) % 4, y, z // 2

    return moves(rule)


COLS_A, COLS_B = to_columns(0), to_columns(1)


def piece_spot(y, z, core, high):
    low_z = (y - z + 4) % 2
    from_core = ((y - z - low_z + 8) // 2 + core) % 2
    return low_z * 4 + high * 2 + from_core


def send(value, pairs):
    return lax.ppermute(value, AXES, pairs)


def column_scale(b):
    squares = jnp.zeros((WIDE, 128), F32)
    for n in range(0, SPEC, 128):
        values = b[:, n : n + 128].astype(F32)
        squares += values * values
    power = lax.dot_general(
        jnp.ones((8, 128), F32), squares, NT, precision=lax.Precision.HIGHEST, preferred_element_type=F32
    )
    return 1.0 / jnp.sqrt(power)


def products(a, b, col_inv, high, out):
    turned = jnp.concatenate([a[:, HALF:], -a[:, :HALF]], axis=1)
    values = a.astype(F32)
    row_inv = 1.0 / jnp.sqrt(jnp.sum(values * values, axis=1, keepdims=True))
    for part, lhs in enumerate((a, turned)):
        cross = lax.dot_general(lhs, b, NT, preferred_element_type=F32)
        scaled = cross * row_inv * col_inv
        out[part, 0, high, 0] = scaled[:SHARD]
        out[part, 0, 1 - high, 0] = scaled[SHARD:]


def half_kernel(where, rows, swapped, *refs):
    pieces, (out, b, col_inv, sems) = refs[:4], refs[-4:]
    step = pl.program_id(0)

    @pl.when(step == 0)
    def _():
        copies = []
        for n, piece in enumerate(pieces):
            at = pl.ds(pl.multiple_of(where[4 + n] * SHARD, SHARD), SHARD)
            copies.append(pltpu.make_async_copy(piece, b.at[at, :], sems.at[n]))
        for copy in copies:
            copy.start()
        for copy in copies:
            copy.wait()
        col_inv[...] = column_scale(b)

    a = jnp.where(step < 3, rows[...], swapped[...])
    products(a, b[...], col_inv[0:1, :], where[2], out)


def half_call(where, rows, swapped, pieces, before, name):
    def place_out(step, where):
        n = lax.rem(step, 3)
        z = lax.rem(where[0] + jnp.where(n == 1, 3, jnp.where(n == 2, 1, 0)), 4)
        return 0, z, 0, where[1] ^ (step // 3), 0, where[3]

    vmem, anywhere = pl.BlockSpec(memory_space=pltpu.VMEM), pl.BlockSpec(memory_space=pl.ANY)
    in_specs = [
        pl.BlockSpec((TILE, SPEC), lambda step, where: (jnp.minimum(step, 2), 0)),
        pl.BlockSpec((TILE, SPEC), lambda step, where: (jnp.maximum(step - 3, 0), 0)),
    ] + [anywhere] * 4
    operands, aliases = (rows, swapped, *[in_hbm(piece) for piece in pieces]), {}
    if before is not None:
        aliases = {1 + len(operands): 0}
        operands = (*operands, before)
        in_specs.append(anywhere)
    return pl.pallas_call(
        half_kernel,
        grid_spec=pltpu.PrefetchScalarGridSpec(
            num_scalar_prefetch=1,
            grid=(6,),
            in_specs=in_specs,
            out_specs=[pl.BlockSpec((2, 1, 2, 1, SHARD, WIDE), place_out), vmem, vmem],
            scratch_shapes=[pltpu.SemaphoreType.DMA((4,))],
        ),
        out_shape=[
            jax.ShapeDtypeStruct(OUT, F32),
            pltpu.VMEM((WIDE, SPEC), BF16),
            pltpu.VMEM((8, WIDE), F32),
        ],
        input_output_aliases=aliases,
        compiler_params=pltpu.CompilerParams(vmem_limit_bytes=16 * 2**20),
        cost_estimate=pl.CostEstimate(flops=3 * 2**30, bytes_accessed=11 * 2**20, transcendentals=2048),
        name=name,
    )(where, *operands)


def facing_kernel(where, rows, swapped, b0, scale0, b1, scale1, before, out):
    step = pl.program_id(0)
    a = jnp.where(step < 2, rows[...], swapped[...])
    even = lax.rem(step, 2) == 0
    b = jnp.where(even, b0[...], b1[...])
    scale = jnp.where(even, scale0[0:1, :], scale1[0:1, :])
    products(a, b, scale, where[2], out)


def facing_call(where, rows, swapped, first, second, before):
    def place_out(step, where):
        return 0, lax.rem(where[0] + 2, 4), 0, where[1] ^ (step // 2), 0, where[3] ^ lax.rem(step, 2)

    vmem, anywhere = pl.BlockSpec(memory_space=pltpu.VMEM), pl.BlockSpec(memory_space=pl.ANY)
    whole = pl.BlockSpec((TILE, SPEC), lambda step, where: (0, 0))
    return pl.pallas_call(
        facing_kernel,
        grid_spec=pltpu.PrefetchScalarGridSpec(
            num_scalar_prefetch=1,
            grid=(4,),
            in_specs=[whole, whole, vmem, vmem, vmem, vmem, anywhere],
            out_specs=pl.BlockSpec((2, 1, 2, 1, SHARD, WIDE), place_out),
        ),
        out_shape=jax.ShapeDtypeStruct(OUT, F32),
        input_output_aliases={7: 0},
        compiler_params=pltpu.CompilerParams(vmem_limit_bytes=16 * 2**20),
        cost_estimate=pl.CostEstimate(flops=2**31, bytes_accessed=8 * 2**20, transcendentals=2048),
        name="facing_rows",
    )(where, rows, swapped, *[in_vmem(v) for v in (*first, *second)], before)


def in_vmem(value):
    return pltpu.with_memory_space_constraint(value, pltpu.VMEM)


def in_hbm(value):
    return pltpu.with_memory_space_constraint(value, pltpu.HBM)


def stack(*values):
    return jnp.stack(values).astype(jnp.int32)


def shards(x):
    row, col = lax.axis_index("row"), lax.axis_index("col")
    low, y, z, high, core = row % 2, row // 2, col // 4, col // 2 % 2, col % 2
    c0, c1, across = send(x, COLS_A), send(x, COLS_B), send(x, ACROSS_X)
    below, above = send(x, Z_UP), send(x, Z_DOWN)
    up0, down0 = send(c0, Y_UP), send(c0, Y_DOWN)
    c1, up0, down0, across, below, above = lax.optimization_barrier((c1, up0, down0, across, below, above))
    down1, up1 = send(c1, Y_DOWN), send(c1, Y_UP)
    below_across, above_across = send(across, Z_UP), send(across, Z_DOWN)
    down1, up1, below_across, above_across = lax.optimization_barrier((down1, up1, below_across, above_across))
    far0, far1 = send(up0, Y_UP), send(down1, Y_DOWN)
    from_below = jnp.concatenate([below, below_across], axis=0)
    from_above = jnp.concatenate([above, above_across], axis=0)
    facing = send(jnp.where(core == 0, from_below, from_above), Z_SPLIT)
    rows = jnp.concatenate([x, across, from_below, from_above], axis=0)
    swapped = send(rows, SWAP_CORE)

    def spots(*steps):
        return [piece_spot((y + up) % 4, z, core, high_x) % 4 for up, high_x in steps]

    near_half = (y + 3 - z + 4) % 2
    where = stack(z, core, high, near_half, *spots((3, low), (3, 1 - low), (1, low), (1, 1 - low)))
    out, *first = half_call(where, rows, swapped, (up0, up1, down0, down1), None, "near_columns")
    out, far0, far1, facing = lax.optimization_barrier((out, far0, far1, facing))
    facing_swapped = send(facing, SWAP_CORE)
    far_where = stack(z, core, high, 1 - near_half, *spots((0, low), (0, 1 - low), (2, low), (2, 1 - low)))
    out, *second = half_call(far_where, rows, swapped, (c0, c1, far0, far1), out, "far_columns")
    out = facing_call(where, facing, facing_swapped, first, second, out)
    return out.reshape(2, 4 * 4 * SHARD, COLS)


def solution(mesh):
    return jax.shard_map(
        shards, mesh=mesh, in_specs=(P(AXES, None),), out_specs=P(None, "row", "col"), check_vma=False
    )
```

time: 366 us -> 76 us (0.21)
  the two profiles are of different devices: /device:TPU:1 before, /device:TPU:5 now
where the time goes in v2:
time: 76 us; the launch traced here: 75.7 us
  starting transfers between devices  35.8 us (47%)
  Pallas kernels  23.2 us (31%)
  waiting for transfers between devices  11.1 us (15%)
  local copies, waits for them, and re-layouts  3.13 us (4%)
  other arithmetic  2.1 us (3%)
    ppermute x16, starting transfers between devices, send(): return lax.ppermute(value, AXES, pairs)  35.8 us
    pallas_call x2, Pallas kernels, half_call(): pl.pallas_call(half_kernel, grid_spec=pltpu.PrefetchScalarGridSpec(num_sc...  16.8 us
    ppermute x16, waiting for transfers between devices, send(): return lax.ppermute(value, AXES, pairs)  11.1 us
    pallas_call x1, Pallas kernels, facing_call(): pl.pallas_call(facing_kernel, grid_spec=pltpu.PrefetchScalarGridSpec(num_...  6.34 us
    unnamed x29, local copies, waits for them, and re-layouts  2.94 us
    select_n x1, other arithmetic, shards(): facing = send(jnp.where(core == 0, from_below, from_above), Z_SPLIT)  2.1 us
  transfers between devices with their start and end apart: 16, of which 5 were waited for; matrix products, arithmetic and copies ran while one was open for 4% of the time, Pallas kernels for 22%

profile of v2, /device:TPU:5, one launch (start us, length us, event | category | flops | bytes accessed | tf_op | source)
XLA Modules:
  0.0 75.7 jit_solution(5410692048765041865)
XLA Ops:
  0.0 5.3 %collective-permute-start.1 = (bf16[128,1024]{1,0:T(8,128)(2,1)}, bf16[128,1024]{1,0:T(8,128)(2,1)S(1)}, u32[]{:S(2)}, u32[]{:S(2)}) collective-permute-start(bf16[128,1024]{1,0:T(8,128)(2,1)} %param.1), channel_id=1, source_target_pairs={{0,0},{1,64},{2,16},{3,80},{4,32},{5,96},{6,48},{7,112},{8,65},{9,... | collective-permute-start | bytes 786440 | tf_op jit(solution)/shard_map/ppermute | solution.py:61
  5.4 1.1 %collective-permute-start.5 = (bf16[128,1024]{1,0:T(8,128)(2,1)}, bf16[128,1024]{1,0:T(8,128)(2,1)S(1)}, u32[]{:S(2)}, u32[]{:S(2)}) collective-permute-start(bf16[128,1024]{1,0:T(8,128)(2,1)} %param.1), channel_id=1, source_target_pairs={{0,4},{1,5},{2,6},{3,7},{4,8},{5,9},{6,10},{7,11},{8,12},{9,13},{1... | collective-permute-start | bytes 786440 | tf_op jit(solution)/shard_map/ppermute | solution.py:61
  6.4 0.3 collective-permute-start.4
  6.7 6.3 %collective-permute-start = (bf16[128,1024]{1,0:T(8,128)(2,1)}, bf16[128,1024]{1,0:T(8,128)(2,1)S(1)}, u32[]{:S(2)}, u32[]{:S(2)}) collective-permute-start(bf16[128,1024]{1,0:T(8,128)(2,1)} %param.1), channel_id=1, source_target_pairs={{0,16},{1,80},{2,0},{3,64},{4,48},{5,112},{6,32},{7,96},{8,81},{9,... | collective-permute-start | bytes 786440 | tf_op jit(solution)/shard_map/ppermute | solution.py:61
  12.9 0.0 collective-permute-start.6
  12.9 0.0 collective-permute-done.1.refs_0_
  13.0 9.0 %collective-permute-start.3 = (bf16[128,1024]{1,0:T(8,128)(2,1)S(1)}, bf16[128,1024]{1,0:T(8,128)(2,1)S(1)}, u32[]{:S(2)}, u32[]{:S(2)}) collective-permute-start(bf16[128,1024]{1,0:T(8,128)(2,1)S(1)} %collective-permute-done.1.refs_0_), channel_id=1, source_target_pairs={{0,96},{1,97},{2,98},{3,99},{4,100},{5,101},{6,102},{7,103},{8,104... | collective-permute-start | bytes 786440 | tf_op jit(solution)/shard_map/ppermute | solution.py:61
  22.0 0.0 collective-permute-done.5
  22.0 0.0 collective-permute-start.2
  22.0 0.0 collective-permute-done.4
  22.0 0.0 collective-permute-done.refs_1_
  22.0 0.0 copy-start.6
  22.0 0.0 collective-permute-done.6
  22.0 0.0 copy-start.2
  22.0 5.3 %collective-permute-done.3.refs_2_ = bf16[128,1024]{1,0:T(8,128)(2,1)S(1)} collective-permute-done((bf16[128,1024]{1,0:T(8,128)(2,1)S(1)}, bf16[128,1024]{1,0:T(8,128)(2,1)S(1)}, u32[]{:S(2)}, u32[]{:S(2)}) %collective-permute-start.3) | collective-permute-done | bytes 262176 | tf_op jit(solution)/shard_map/ppermute | solution.py:61
  27.3 0.0 copy-done.5
  27.3 3.1 %collective-permute-done.2.refs_0_ = bf16[128,1024]{1,0:T(8,128)(2,1)S(1)} collective-permute-done((bf16[128,1024]{1,0:T(8,128)(2,1)S(1)}, bf16[128,1024]{1,0:T(8,128)(2,1)S(1)}, u32[]{:S(2)}, u32[]{:S(2)}) %collective-permute-start.2) | collective-permute-done | bytes 262176 | tf_op jit(solution)/shard_map/ppermute | solution.py:61
  30.4 0.0 copy-done.8
  30.4 0.0 collective-permute-start.10
  30.4 1.5 %collective-permute-start.9 = (bf16[128,1024]{1,0:T(8,128)(2,1)S(1)}, bf16[128,1024]{1,0:T(8,128)(2,1)S(1)}, u32[]{:S(2)}, u32[]{:S(2)}) collective-permute-start(bf16[128,1024]{1,0:T(8,128)(2,1)S(1)} %collective-permute-done.4), channel_id=1, source_target_pairs={{0,4},{1,5},{2,6},{3,7},{4,8},{5,9},{6,10},{7,11},{8,12},{9,13},{1... | collective-permute-start | bytes 786440 | tf_op jit(solution)/shard_map/ppermute | solution.py:61
  31.8 0.3 collective-permute-start.8
  32.2 2.3 %collective-permute-start.7 = (bf16[128,1024]{1,0:T(8,128)(2,1)S(1)}, bf16[128,1024]{1,0:T(8,128)(2,1)S(1)}, u32[]{:S(2)}, u32[]{:S(2)}) collective-permute-start(bf16[128,1024]{1,0:T(8,128)(2,1)S(1)} %collective-permute-done.refs_1_), channel_id=1, source_target_pairs={{0,96},{1,97},{2,98},{3,99},{4,100},{5,101},{6,102},{7,103},{8,104... | collective-permute-start | bytes 786440 | tf_op jit(solution)/shard_map/ppermute | solution.py:61
  34.5 1.0 %constant_dynamic-update-slice_fusion.5 = bf16[768,1024]{1,0:T(8,128)(2,1)S(1)} fusion(bf16[128,1024]{1,0:T(8,128)(2,1)} %param.1), kind=kLoop, calls=%fused_computation.6 | loop fusion | bytes 524288
  35.6 1.1 %collective-permute-done.10 = bf16[128,1024]{1,0:T(8,128)(2,1)S(1)} collective-permute-done((bf16[128,1024]{1,0:T(8,128)(2,1)S(1)}, bf16[128,1024]{1,0:T(8,128)(2,1)S(1)}, u32[]{:S(2)}, u32[]{:S(2)}) %collective-permute-start.10) | collective-permute-done | bytes 262176 | tf_op jit(solution)/shard_map/ppermute | solution.py:61
  36.7 0.2 collective-permute-done.9
  36.9 1.4 %collective-permute-done.8.refs_1_ = bf16[128,1024]{1,0:T(8,128)(2,1)S(1)} collective-permute-done((bf16[128,1024]{1,0:T(8,128)(2,1)S(1)}, bf16[128,1024]{1,0:T(8,128)(2,1)S(1)}, u32[]{:S(2)}, u32[]{:S(2)}) %collective-permute-start.8) | collective-permute-done | bytes 262176 | tf_op jit(solution)/shard_map/ppermute | solution.py:61
  38.3 0.0 collective-permute-done.7.refs_3_
  38.3 0.0 copy-done.6
  38.4 0.0 copy-done.2
  38.4 0.6 copy-done.10
  39.0 3.8 %collective-permute-start.11 = (bf16[768,1024]{1,0:T(8,128)(2,1)S(1)}, bf16[768,1024]{1,0:T(8,128)(2,1)S(1)}, u32[]{:S(2)}, u32[]{:S(2)}) collective-permute-start(bf16[768,1024]{1,0:T(8,128)(2,1)S(1)} %constant_dynamic-update-slice_fusion.rows), channel_id=1, source_target_pairs={{0,1},{1,0},{2,3},{3,2},{4,5},{5,4},{6,7},{7,6},{8,9},{9,8},{10,11... | collective-permute-start | bytes 4718600 | tf_op jit(solution)/shard_map/ppermute | solution.py:61
  42.8 2.1 %maximum_select_fusion = bf16[256,1024]{1,0:T(8,128)(2,1)} fusion(bf16[128,1024]{1,0:T(8,128)(2,1)} %copy-done.4, bf16[128,1024]{1,0:T(8,128)(2,1)S(1)} %collective-permute-done.5, bf16[128,1024]{1,0:T(8,128)(2,1)} %copy-done.3, bf16[128,1024]{1,0:T(8,128)(2,1)} %copy-done.2, pred[]{:T(512)S(6)} %eq.40), kind=kLoop, calls=%fused_computation | loop fusion | flops 2359296 | bytes 1572865 | tf_op jit(solution)/shard_map/jit(_where)/select_n | solution.py:199
  44.9 2.8 %collective-permute-start.14 = (bf16[256,1024]{1,0:T(8,128)(2,1)}, bf16[256,1024]{1,0:T(8,128)(2,1)}, u32[]{:S(2)}, u32[]{:S(2)}) collective-permute-start(bf16[256,1024]{1,0:T(8,128)(2,1)} %maximum_select_fusion), channel_id=1, source_target_pairs={{0,4},{1,13},{2,6},{3,15},{4,8},{5,1},{6,10},{7,3},{8,12},{9,5},{1... | collective-permute-start | bytes 1572872 | tf_op jit(solution)/shard_map/ppermute | solution.py:61
  47.7 0.1 stack.56.where
  47.8 0.0 collective-permute-start.12
  47.8 3.0 %collective-permute-start.13 = (bf16[128,1024]{1,0:T(8,128)(2,1)}, bf16[128,1024]{1,0:T(8,128)(2,1)}, u32[]{:S(2)}, u32[]{:S(2)}) collective-permute-start(bf16[128,1024]{1,0:T(8,128)(2,1)} %copy-done.10), channel_id=1, source_target_pairs={{0,96},{1,97},{2,98},{3,99},{4,100},{5,101},{6,102},{7,103},{8,104... | collective-permute-start | bytes 786440 | tf_op jit(solution)/shard_map/ppermute | solution.py:61
  50.8 0.0 collective-permute-done.11.swapped
  50.8 8.4 %near_columns.1 = (f32[2,4,2,2,128,1024]{5,4,3,2,1,0:T(8,128)}, bf16[512,1024]{1,0:T(8,128)(2,1)S(1)}, f32[8,512]{1,0:T(8,128)S(1)}) custom-call(s32[8]{0:T(128)S(1)} %stack.56.where, bf16[768,1024]{1,0:T(8,128)(2,1)S(1)} %constant_dynamic-update-slice_fusion.rows, bf16[768,1024]{1,0:T(8,128)(2,1)S(1)} %collective-permute-done.11.swapped, ...), custom_call_target="tpu_custom_call" | custom-call | flops 3221225472 | bytes 11534336 | tf_op jit(solution)/shard_map/near_columns/pallas_call | solution.py:122
  59.2 1.0 %copy-done = bf16[512,1024]{1,0:T(8,128)(2,1)} copy-done((bf16[512,1024]{1,0:T(8,128)(2,1)}, bf16[512,1024]{1,0:T(8,128)(2,1)S(1)}, u32[]{:S(2)}) %copy-start) | copy-done | bytes 1048600
  60.2 0.0 collective-permute-done.12.refs_2_
  60.2 0.0 collective-permute-done.13.refs_3_
  60.2 0.0 collective-permute-done.14.rows
  60.2 0.1 collective-permute-start.15
  60.6 0.1 stack.62.where
  60.6 0.3 copy-done.7
  60.9 8.4 %far_columns.1 = (f32[2,4,2,2,128,1024]{5,4,3,2,1,0:T(8,128)}, bf16[512,1024]{1,0:T(8,128)(2,1)S(1)}, f32[8,512]{1,0:T(8,128)S(1)}) custom-call(s32[8]{0:T(128)S(1)} %stack.62.where, bf16[768,1024]{1,0:T(8,128)(2,1)S(1)} %constant_dynamic-update-slice_fusion.rows, ...), custom_call_target="tpu_custom_call", output_to_operand_aliasing={{0}: (7, {})} | custom-call | flops 3221225472 | bytes 11534336 | tf_op jit(solution)/shard_map/far_columns/pallas_call | solution.py:122
  69.4 0.0 collective-permute-done.15.swapped
  69.4 6.3 %facing_rows.1 = f32[2,4,2,2,128,1024]{5,4,3,2,1,0:T(8,128)} custom-call(s32[8]{0:T(128)S(1)} %stack.56.where, bf16[256,1024]{1,0:T(8,128)(2,1)} %collective-permute-done.14.rows, bf16[256,1024]{1,0:T(8,128)(2,1)} %collective-permute-done.15.swapped, bf16[512,1024]{1,0:T(8,128)(2,1)S(1)} %copy-done.1, ...), custom_call_target="tpu_custom_call", output_to_operand_aliasing={{}: (7, {})} | custom-call | flops 2147483648 | bytes 8388608 | tf_op jit(solution)/shard_map/facing_rows/pallas_call | solution.py:158
  (20 shorter events, 0.1 us)
Async XLA Ops:
  0.0 12.9 %collective-permute-start.1 = (bf16[128,1024]{1,0:T(8,128)(2,1)}, bf16[128,1024]{1,0:T(8,128)(2,1)S(1)}, u32[]{:S(2)}, u32[]{:S(2)}) collective-permute-start(bf16[128,1024]{1,0:T(8,128)(2,1)} %param.1), channel_id=1, source_target_pairs={{0,0},{1,64},{2,16},{3,80},{4,32},{5,96},{6,48},{7,112},{8,65},{9,... | collective-permute-start | bytes 786440 | tf_op jit(solution)/shard_map/ppermute | solution.py:61
  5.4 16.6 %collective-permute-start.5 = (bf16[128,1024]{1,0:T(8,128)(2,1)}, bf16[128,1024]{1,0:T(8,128)(2,1)S(1)}, u32[]{:S(2)}, u32[]{:S(2)}) collective-permute-start(bf16[128,1024]{1,0:T(8,128)(2,1)} %param.1), channel_id=1, source_target_pairs={{0,4},{1,5},{2,6},{3,7},{4,8},{5,9},{6,10},{7,11},{8,12},{9,13},{1... | collective-permute-start | bytes 786440 | tf_op jit(solution)/shard_map/ppermute | solution.py:61
  6.4 15.6 %collective-permute-start.4 = (bf16[128,1024]{1,0:T(8,128)(2,1)}, bf16[128,1024]{1,0:T(8,128)(2,1)S(1)}, u32[]{:S(2)}, u32[]{:S(2)}) collective-permute-start(bf16[128,1024]{1,0:T(8,128)(2,1)} %param.1), channel_id=1, source_target_pairs={{0,2},{1,3},{2,0},{3,1},{4,6},{5,7},{6,4},{7,5},{8,10},{9,11},{10,... | collective-permute-start | bytes 786440 | tf_op jit(solution)/shard_map/ppermute | solution.py:61
  6.7 15.3 %collective-permute-start = (bf16[128,1024]{1,0:T(8,128)(2,1)}, bf16[128,1024]{1,0:T(8,128)(2,1)S(1)}, u32[]{:S(2)}, u32[]{:S(2)}) collective-permute-start(bf16[128,1024]{1,0:T(8,128)(2,1)} %param.1), channel_id=1, source_target_pairs={{0,16},{1,80},{2,0},{3,64},{4,48},{5,112},{6,32},{7,96},{8,81},{9,... | collective-permute-start | bytes 786440 | tf_op jit(solution)/shard_map/ppermute | solution.py:61
  12.9 9.1 %collective-permute-start.6 = (bf16[128,1024]{1,0:T(8,128)(2,1)}, bf16[128,1024]{1,0:T(8,128)(2,1)S(1)}, u32[]{:S(2)}, u32[]{:S(2)}) collective-permute-start(bf16[128,1024]{1,0:T(8,128)(2,1)} %param.1), channel_id=1, source_target_pairs={{0,12},{1,13},{2,14},{3,15},{4,0},{5,1},{6,2},{7,3},{8,4},{9,5},{1... | collective-permute-start | bytes 786440 | tf_op jit(solution)/shard_map/ppermute | solution.py:61
  12.9 14.3 %copy-start.5 = (bf16[128,1024]{1,0:T(8,128)(2,1)}, bf16[128,1024]{1,0:T(8,128)(2,1)S(1)}, u32[]{:S(2)}) copy-start(bf16[128,1024]{1,0:T(8,128)(2,1)S(1)} %collective-permute-done.1.refs_0_) | copy-start | bytes 786436
  13.0 14.3 %collective-permute-start.3 = (bf16[128,1024]{1,0:T(8,128)(2,1)S(1)}, bf16[128,1024]{1,0:T(8,128)(2,1)S(1)}, u32[]{:S(2)}, u32[]{:S(2)}) collective-permute-start(bf16[128,1024]{1,0:T(8,128)(2,1)S(1)} %collective-permute-done.1.refs_0_), channel_id=1, source_target_pairs={{0,96},{1,97},{2,98},{3,99},{4,100},{5,101},{6,102},{7,103},{8,104... | collective-permute-start | bytes 786440 | tf_op jit(solution)/shard_map/ppermute | solution.py:61
  22.0 8.4 %collective-permute-start.2 = (bf16[128,1024]{1,0:T(8,128)(2,1)S(1)}, bf16[128,1024]{1,0:T(8,128)(2,1)S(1)}, u32[]{:S(2)}, u32[]{:S(2)}) collective-permute-start(bf16[128,1024]{1,0:T(8,128)(2,1)S(1)} %collective-permute-done.1.refs_0_), channel_id=1, source_target_pairs={{0,32},{1,33},{2,34},{3,35},{4,36},{5,37},{6,38},{7,39},{8,40},{9,... | collective-permute-start | bytes 786440 | tf_op jit(solution)/shard_map/ppermute | solution.py:61
  22.0 16.3 %copy-start.6 = (bf16[128,1024]{1,0:T(8,128)(2,1)}, bf16[128,1024]{1,0:T(8,128)(2,1)S(1)}, u32[]{:S(2)}) copy-start(bf16[128,1024]{1,0:T(8,128)(2,1)S(1)} %collective-permute-done.refs_1_) | copy-start | bytes 786436
  22.0 16.3 %copy-start.2 = (bf16[128,1024]{1,0:T(8,128)(2,1)}, bf16[128,1024]{1,0:T(8,128)(2,1)S(1)}, u32[]{:S(2)}) copy-start(bf16[128,1024]{1,0:T(8,128)(2,1)S(1)} %collective-permute-done.6) | copy-start | bytes 786436
  27.3 3.1 %copy-start.8 = (bf16[128,1024]{1,0:T(8,128)(2,1)}, bf16[128,1024]{1,0:T(8,128)(2,1)S(1)}, u32[]{:S(2)}) copy-start(bf16[128,1024]{1,0:T(8,128)(2,1)S(1)} %collective-permute-done.3.refs_2_) | copy-start | bytes 786436
  30.4 8.0 %copy-start.9 = (bf16[128,1024]{1,0:T(8,128)(2,1)}, bf16[128,1024]{1,0:T(8,128)(2,1)S(1)}, u32[]{:S(2)}) copy-start(bf16[128,1024]{1,0:T(8,128)(2,1)S(1)} %collective-permute-done.2.refs_0_) | copy-start | bytes 786436
  30.4 6.3 %collective-permute-start.10 = (bf16[128,1024]{1,0:T(8,128)(2,1)S(1)}, bf16[128,1024]{1,0:T(8,128)(2,1)S(1)}, u32[]{:S(2)}, u32[]{:S(2)}) collective-permute-start(bf16[128,1024]{1,0:T(8,128)(2,1)S(1)} %collective-permute-done.4), channel_id=1, source_target_pairs={{0,12},{1,13},{2,14},{3,15},{4,0},{5,1},{6,2},{7,3},{8,4},{9,5},{1... | collective-permute-start | bytes 786440 | tf_op jit(solution)/shard_map/ppermute | solution.py:61
  30.4 6.5 %collective-permute-start.9 = (bf16[128,1024]{1,0:T(8,128)(2,1)S(1)}, bf16[128,1024]{1,0:T(8,128)(2,1)S(1)}, u32[]{:S(2)}, u32[]{:S(2)}) collective-permute-start(bf16[128,1024]{1,0:T(8,128)(2,1)S(1)} %collective-permute-done.4), channel_id=1, source_target_pairs={{0,4},{1,5},{2,6},{3,7},{4,8},{5,9},{6,10},{7,11},{8,12},{9,13},{1... | collective-permute-start | bytes 786440 | tf_op jit(solution)/shard_map/ppermute | solution.py:61
  31.8 6.4 %collective-permute-start.8 = (bf16[128,1024]{1,0:T(8,128)(2,1)S(1)}, bf16[128,1024]{1,0:T(8,128)(2,1)S(1)}, u32[]{:S(2)}, u32[]{:S(2)}) collective-permute-start(bf16[128,1024]{1,0:T(8,128)(2,1)S(1)} %collective-permute-done.refs_1_), channel_id=1, source_target_pairs={{0,32},{1,33},{2,34},{3,35},{4,36},{5,37},{6,38},{7,39},{8,40},{9,... | collective-permute-start | bytes 786440 | tf_op jit(solution)/shard_map/ppermute | solution.py:61
  32.2 6.1 %collective-permute-start.7 = (bf16[128,1024]{1,0:T(8,128)(2,1)S(1)}, bf16[128,1024]{1,0:T(8,128)(2,1)S(1)}, u32[]{:S(2)}, u32[]{:S(2)}) collective-permute-start(bf16[128,1024]{1,0:T(8,128)(2,1)S(1)} %collective-permute-done.refs_1_), channel_id=1, source_target_pairs={{0,96},{1,97},{2,98},{3,99},{4,100},{5,101},{6,102},{7,103},{8,104... | collective-permute-start | bytes 786440 | tf_op jit(solution)/shard_map/ppermute | solution.py:61
  36.7 1.7 %copy-start.3 = (bf16[128,1024]{1,0:T(8,128)(2,1)}, bf16[128,1024]{1,0:T(8,128)(2,1)S(1)}, u32[]{:S(2)}) copy-start(bf16[128,1024]{1,0:T(8,128)(2,1)S(1)} %collective-permute-done.10) | copy-start | bytes 786436
  36.9 1.5 %copy-start.4 = (bf16[128,1024]{1,0:T(8,128)(2,1)}, bf16[128,1024]{1,0:T(8,128)(2,1)S(1)}, u32[]{:S(2)}) copy-start(bf16[128,1024]{1,0:T(8,128)(2,1)S(1)} %collective-permute-done.9) | copy-start | bytes 786436
  38.3 4.5 %copy-start.11 = (bf16[128,1024]{1,0:T(8,128)(2,1)}, bf16[128,1024]{1,0:T(8,128)(2,1)S(1)}, u32[]{:S(2)}) copy-start(bf16[128,1024]{1,0:T(8,128)(2,1)S(1)} %collective-permute-done.8.refs_1_) | copy-start | bytes 786436
  38.3 0.7 copy-start.10
  39.0 11.8 %collective-permute-start.11 = (bf16[768,1024]{1,0:T(8,128)(2,1)S(1)}, bf16[768,1024]{1,0:T(8,128)(2,1)S(1)}, u32[]{:S(2)}, u32[]{:S(2)}) collective-permute-start(bf16[768,1024]{1,0:T(8,128)(2,1)S(1)} %constant_dynamic-update-slice_fusion.rows), channel_id=1, source_target_pairs={{0,1},{1,0},{2,3},{3,2},{4,5},{5,4},{6,7},{7,6},{8,9},{9,8},{10,11... | collective-permute-start | bytes 4718600 | tf_op jit(solution)/shard_map/ppermute | solution.py:61
  44.9 15.3 %collective-permute-start.14 = (bf16[256,1024]{1,0:T(8,128)(2,1)}, bf16[256,1024]{1,0:T(8,128)(2,1)}, u32[]{:S(2)}, u32[]{:S(2)}) collective-permute-start(bf16[256,1024]{1,0:T(8,128)(2,1)} %maximum_select_fusion), channel_id=1, source_target_pairs={{0,4},{1,13},{2,6},{3,15},{4,8},{5,1},{6,10},{7,3},{8,12},{9,5},{1... | collective-permute-start | bytes 1572872 | tf_op jit(solution)/shard_map/ppermute | solution.py:61
  47.8 12.4 %collective-permute-start.12 = (bf16[128,1024]{1,0:T(8,128)(2,1)}, bf16[128,1024]{1,0:T(8,128)(2,1)S(1)}, u32[]{:S(2)}, u32[]{:S(2)}) collective-permute-start(bf16[128,1024]{1,0:T(8,128)(2,1)} %copy-done.9), channel_id=1, source_target_pairs={{0,32},{1,33},{2,34},{3,35},{4,36},{5,37},{6,38},{7,39},{8,40},{9,... | collective-permute-start | bytes 786440 | tf_op jit(solution)/shard_map/ppermute | solution.py:61
  47.8 12.4 %collective-permute-start.13 = (bf16[128,1024]{1,0:T(8,128)(2,1)}, bf16[128,1024]{1,0:T(8,128)(2,1)}, u32[]{:S(2)}, u32[]{:S(2)}) collective-permute-start(bf16[128,1024]{1,0:T(8,128)(2,1)} %copy-done.10), channel_id=1, source_target_pairs={{0,96},{1,97},{2,98},{3,99},{4,100},{5,101},{6,102},{7,103},{8,104... | collective-permute-start | bytes 786440 | tf_op jit(solution)/shard_map/ppermute | solution.py:61
  59.2 1.0 %copy-start = (bf16[512,1024]{1,0:T(8,128)(2,1)}, bf16[512,1024]{1,0:T(8,128)(2,1)S(1)}, u32[]{:S(2)}) copy-start(bf16[512,1024]{1,0:T(8,128)(2,1)S(1)} %get-tuple-element.37.b0) | copy-start | bytes 3145732
  60.2 0.7 copy-start.7
  60.2 9.1 %collective-permute-start.15 = (bf16[256,1024]{1,0:T(8,128)(2,1)}, bf16[256,1024]{1,0:T(8,128)(2,1)}, u32[]{:S(2)}, u32[]{:S(2)}) collective-permute-start(bf16[256,1024]{1,0:T(8,128)(2,1)} %collective-permute-done.14.rows), channel_id=1, source_target_pairs={{0,1},{1,0},{2,3},{3,2},{4,5},{5,4},{6,7},{7,6},{8,9},{9,8},{10,11... | collective-permute-start | bytes 1572872 | tf_op jit(solution)/shard_map/ppermute | solution.py:61
  60.9 8.4 %copy-start.1 = (bf16[512,1024]{1,0:T(8,128)(2,1)S(1)}, bf16[512,1024]{1,0:T(8,128)(2,1)}, u32[]{:S(2)}) copy-start(bf16[512,1024]{1,0:T(8,128)(2,1)} %copy-done) | copy-start | bytes 3145732

commit v3 on v2

v3 whole, which is shorter than its diff:
```python
import jax
import jax.numpy as jnp
from jax import lax
from jax.experimental import pallas as pl
from jax.experimental.pallas import tpu as pltpu
from jax.sharding import PartitionSpec as P

TAPERS = 8
BINS = 64
HALF = TAPERS * BINS
SPEC = 2 * HALF
AXES = ("row", "col")
NT = (((1,), (1,)), ((), ()))
F32, BF16 = jnp.float32, jnp.bfloat16
SHARD = 128
COLS = 8 * SHARD
WIDE = COLS // 2
OUT = (2, 4, 2, 2, SHARD, COLS)
TILE = 2 * SHARD


def place(i):
    row, col = divmod(i, 16)
    return (col // 2 % 2) * 2 + row % 2, row // 2, col // 4, col % 2


def number(x, y, z, core):
    return (y * 2 + x % 2) * 16 + z * 4 + (x // 2) * 2 + core


def moves(rule):
    return [(i, number(*rule(*place(i)))) for i in range(128)]


SWAP_CORE = moves(lambda x, y, z, c: (x, y, z, 1 - c))
ACROSS_X = moves(lambda x, y, z, c: ((x + 2) % 4, y, z, c))
Y_UP = moves(lambda x, y, z, c: (x, (y + 1) % 4, z, c))
Y_DOWN = moves(lambda x, y, z, c: (x, (y + 3) % 4, z, c))
Z_UP = moves(lambda x, y, z, c: (x, y, (z + 1) % 4, c))
Z_DOWN = moves(lambda x, y, z, c: (x, y, (z + 3) % 4, c))
Z_SPLIT_CROSS = moves(lambda x, y, z, c: (x, y, (z + 1 + 2 * c) % 4, 1 - c))
Z_SPLIT = moves(lambda x, y, z, c: (x, y, (z + 1 + 2 * c) % 4, c))


def to_columns(flip):
    def rule(x, y, z, c):
        return 2 * (x % 2) + (x // 2 ^ flip), (y + z + 2 * c) % 4, y, z // 2

    return moves(rule)


COLS_A, COLS_B = to_columns(0), to_columns(1)


def piece_spot(y, z, core, high):
    low_z = (y - z + 4) % 2
    from_core = ((y - z - low_z + 8) // 2 + core) % 2
    return low_z * 4 + high * 2 + from_core


def send(value, pairs):
    return lax.ppermute(value, AXES, pairs)


def column_scale(b):
    squares = jnp.zeros((WIDE, 128), F32)
    for n in range(0, SPEC, 128):
        values = b[:, n : n + 128].astype(F32)
        squares += values * values
    power = lax.dot_general(
        jnp.ones((8, 128), F32), squares, NT, precision=lax.Precision.HIGHEST, preferred_element_type=F32
    )
    return 1.0 / jnp.sqrt(power)


def products(rows, swapped, columns, core, out):
    a = jnp.concatenate([rows, swapped], axis=0)
    turned = jnp.concatenate([a[:, HALF:], -a[:, :HALF]], axis=1)
    values = a.astype(F32)
    row_inv = 1.0 / jnp.sqrt(jnp.sum(values * values, axis=1, keepdims=True))
    for b, col_inv, at in columns:
        for part, lhs in enumerate((a, turned)):
            cross = lax.dot_general(lhs, b[...], NT, preferred_element_type=F32)
            scaled = cross * row_inv * col_inv[0:1, :]
            out[part, 0, 0, core, :, at] = scaled[:SHARD]
            out[part, 0, 0, 1 - core, :, at] = scaled[SHARD:]


def half_kernel(where, rows, swapped, *refs):
    out, b, col_inv, sems = refs[-4:]
    pieces = [ref.at[pl.ds(n, SHARD)] for ref in refs[:-4] if len(ref.shape) == 2 for n in range(0, ref.shape[0], SHARD)]

    @pl.when(pl.program_id(0) == 0)
    def _():
        spots = [pl.ds(pl.multiple_of(where[4 + n] * SHARD, SHARD), SHARD) for n in range(4)]
        copies = [pltpu.make_async_copy(pieces[n], b.at[spots[n], :], sems.at[n]) for n in range(4)]
        for copy in copies:
            copy.start()
        for copy in copies:
            copy.wait()
        col_inv[...] = column_scale(b)

    products(rows[...], swapped[...], ((b, col_inv, slice(None)),), where[2], out)


def z_of(step, where):
    return lax.rem(where[0] + jnp.where(step == 1, 3, jnp.where(step == 2, 1, jnp.where(step == 3, 2, 0))), 4)


SHARD_SPEC = pl.BlockSpec((SHARD, SPEC), lambda step, where: (step, 0))


def half_call(where, rows, swapped, pieces, before, name):
    def place_out(step, where):
        return 0, z_of(step, where), where[1], 0, 0, where[3]

    vmem, anywhere = pl.BlockSpec(memory_space=pltpu.VMEM), pl.BlockSpec(memory_space=pl.ANY)
    in_specs = [SHARD_SPEC, SHARD_SPEC] + [anywhere] * len(pieces)
    operands, aliases = (rows, swapped, *[in_hbm(piece) for piece in pieces]), {}
    if before is not None:
        aliases = {1 + len(operands): 0}
        operands = (*operands, before)
        in_specs.append(anywhere)
    return pl.pallas_call(
        half_kernel,
        grid_spec=pltpu.PrefetchScalarGridSpec(
            num_scalar_prefetch=1,
            grid=(4,),
            in_specs=in_specs,
            out_specs=[pl.BlockSpec((2, 1, 1, 2, SHARD, WIDE), place_out), vmem, vmem],
            scratch_shapes=[pltpu.SemaphoreType.DMA((4,))],
        ),
        out_shape=[
            jax.ShapeDtypeStruct(OUT, F32),
            (pltpu.HBM if before is None else jax.ShapeDtypeStruct)((WIDE, SPEC), BF16),
            jax.ShapeDtypeStruct((8, WIDE), F32),
        ],
        input_output_aliases=aliases,
        compiler_params=pltpu.CompilerParams(vmem_limit_bytes=16 * 2**20),
        cost_estimate=pl.CostEstimate(flops=2**31, bytes_accessed=7 * 2**20, transcendentals=2048),
        name=name,
    )(where, *operands)


def last_kernel(where, rows3, facing, swapped3, swapped_facing, b0, scale0, b1, scale1, before, out):
    near = pl.program_id(0) < 3
    rows = jnp.where(near, rows3[...], facing[...])
    swapped = jnp.where(near, swapped3[...], swapped_facing[...])
    at0 = pl.ds(pl.multiple_of(where[3] * WIDE, WIDE), WIDE)
    at1 = pl.ds(pl.multiple_of((1 - where[3]) * WIDE, WIDE), WIDE)
    products(rows, swapped, ((b0, scale0, at0), (b1, scale1, at1)), where[2], out)


def last_call(where, rows, first, second, before):
    def place_out(step, where):
        return 0, z_of(step, where), 1 - where[1], 0, 0, 0

    vmem, anywhere = pl.BlockSpec(memory_space=pltpu.VMEM), pl.BlockSpec(memory_space=pl.ANY)
    first_spec = pl.BlockSpec((WIDE, SPEC), lambda step, where: (0, 0))
    of_three = pl.BlockSpec((SHARD, SPEC), lambda step, where: (jnp.minimum(step, 2), 0))
    whole = pl.BlockSpec((SHARD, SPEC), lambda step, where: (0, 0))
    return pl.pallas_call(
        last_kernel,
        grid_spec=pltpu.PrefetchScalarGridSpec(
            num_scalar_prefetch=1,
            grid=(4,),
            in_specs=[of_three, whole, of_three, whole, first_spec, vmem, vmem, vmem, anywhere],
            out_specs=pl.BlockSpec((2, 1, 1, 2, SHARD, COLS), place_out),
        ),
        out_shape=jax.ShapeDtypeStruct(OUT, F32),
        input_output_aliases={9: 0},
        compiler_params=pltpu.CompilerParams(vmem_limit_bytes=16 * 2**20),
        cost_estimate=pl.CostEstimate(flops=2**32, bytes_accessed=12 * 2**20, transcendentals=2048),
        name="across_rows",
    )(where, *rows, in_hbm(first[0]), first[1], *second, before)


def in_hbm(value):
    return pltpu.with_memory_space_constraint(value, pltpu.HBM)


def stack(*values):
    return jnp.stack(values).astype(jnp.int32)


def together(*values):
    return lax.optimization_barrier(values)


def family(*shards):
    return jnp.concatenate(shards, axis=0)


def shards(x):
    row, col = lax.axis_index("row"), lax.axis_index("col")
    low, y, z, high, core = row % 2, row // 2, col // 4, col // 2 % 2, col % 2

    def places(half, *steps):
        return stack(z, high, core, half, *[piece_spot((y + up) % 4, z, core, hx) % 4 for up, hx in steps])

    near_half = (y - z + 3) % 2
    where = places(near_half, (3, low), (3, 1 - low), (1, low), (1, 1 - low))
    where_far = places(1 - near_half, (0, low), (0, 1 - low), (2, low), (2, 1 - low))
    a0, across, below, above, b0 = send(x, COLS_A), send(x, ACROSS_X), send(x, Z_UP), send(x, Z_DOWN), send(x, COLS_B)
    a0, b0 = together(a0, b0)
    own = family(a0, b0)
    up, down = send(own, Y_UP), send(own, Y_DOWN)
    facing = send(jnp.where(core == 0, below, above), Z_SPLIT)
    below_across, above_across = send(across, Z_UP), send(across, Z_DOWN)
    onward = jnp.where(core == 0, below_across, above_across)
    rows_across = family(across, below_across, above_across)
    up, down, facing, rows_across, onward, up_a, down_b = together(up, down, facing, rows_across, onward, up[:SHARD], down[SHARD:])
    far0, far1 = send(up_a, Y_UP), send(down_b, Y_DOWN)
    rows = family(x, below, above, facing)
    swapped = send(rows, SWAP_CORE)
    facing_across = send(onward, Z_SPLIT)
    out, *first = half_call(where, rows, swapped, (up, down), None, "own_rows_near")
    out, facing_across, far0, far1 = together(out, facing_across, far0, far1)
    swapped_across = send(rows_across, SWAP_CORE)
    facing_swapped = send(facing_across, SWAP_CORE)
    out, *second = half_call(where_far, rows, swapped, (own, far0, far1), out, "own_rows_far")
    out = last_call(where, (rows_across, facing_across, swapped_across, facing_swapped), first, second, out)
    return out.reshape(2, 4 * 4 * SHARD, COLS)


def solution(mesh):
    return jax.shard_map(
        shards, mesh=mesh, in_specs=(P(AXES, None),), out_specs=P(None, "row", "col"), check_vma=False
    )
```

time: 76 us -> 66.3 us (0.87)
  the two profiles are of different devices: /device:TPU:5 before, /device:TPU:1 now
where the time goes in v3:
time: 66.3 us; the launch traced here: 66.1 us
  starting transfers between devices  31.6 us (48%)
  Pallas kernels  22.1 us (33%)
  waiting for transfers between devices  7.83 us (12%)
  local copies, waits for them, and re-layouts  3.48 us (5%)
  other arithmetic  0.84 us (1%)
    ppermute x16, starting transfers between devices, send(): return lax.ppermute(value, AXES, pairs)  31.6 us
    pallas_call x2, Pallas kernels, half_call(): pl.pallas_call(half_kernel, grid_spec=pltpu.PrefetchScalarGridSpec(num_sc...  13.6 us
    pallas_call x1, Pallas kernels, last_call(): pl.pallas_call(last_kernel, grid_spec=pltpu.PrefetchScalarGridSpec(num_sc...  8.57 us
    ppermute x16, waiting for transfers between devices, send(): return lax.ppermute(value, AXES, pairs)  7.83 us
    unnamed x11, local copies, waits for them, and re-layouts  1.73 us
  transfers between devices with their start and end apart: 16, of which 3 were waited for; matrix products, arithmetic and copies ran while one was open for 5% of the time, Pallas kernels for 21%

profile of v3, /device:TPU:1, one launch (start us, length us, event | category | flops | bytes accessed | tf_op | source)
XLA Modules:
  0.0 66.1 jit_solution(10039203343894302872)
XLA Ops:
  0.0 6.2 %collective-permute-start = (bf16[128,1024]{1,0:T(8,128)(2,1)}, bf16[128,1024]{1,0:T(8,128)(2,1)S(1)}, u32[]{:S(2)}, u32[]{:S(2)}) collective-permute-start(bf16[128,1024]{1,0:T(8,128)(2,1)} %param.1), channel_id=1, source_target_pairs={{0,0},{1,64},{2,16},{3,80},{4,32},{5,96},{6,48},{7,112},{8,65},{9,... | collective-permute-start | bytes 786440 | tf_op jit(solution)/shard_map/ppermute | solution.py:62
  6.2 5.8 %collective-permute-start.1 = (bf16[128,1024]{1,0:T(8,128)(2,1)}, bf16[128,1024]{1,0:T(8,128)(2,1)S(1)}, u32[]{:S(2)}, u32[]{:S(2)}) collective-permute-start(bf16[128,1024]{1,0:T(8,128)(2,1)} %param.1), channel_id=1, source_target_pairs={{0,16},{1,80},{2,0},{3,64},{4,48},{5,112},{6,32},{7,96},{8,81},{9,... | collective-permute-start | bytes 786440 | tf_op jit(solution)/shard_map/ppermute | solution.py:62
  12.0 0.8 %collective-permute-start.7 = (bf16[128,1024]{1,0:T(8,128)(2,1)}, bf16[128,1024]{1,0:T(8,128)(2,1)S(1)}, u32[]{:S(2)}, u32[]{:S(2)}) collective-permute-start(bf16[128,1024]{1,0:T(8,128)(2,1)} %param.1), channel_id=1, source_target_pairs={{0,2},{1,3},{2,0},{3,1},{4,6},{5,7},{6,4},{7,5},{8,10},{9,11},{10,... | collective-permute-start | bytes 786440 | tf_op jit(solution)/shard_map/ppermute | solution.py:62
  12.9 1.2 %collective-permute-start.4 = (bf16[128,1024]{1,0:T(8,128)(2,1)}, bf16[128,1024]{1,0:T(8,128)(2,1)S(1)}, u32[]{:S(2)}, u32[]{:S(2)}) collective-permute-start(bf16[128,1024]{1,0:T(8,128)(2,1)} %param.1), channel_id=1, source_target_pairs={{0,4},{1,5},{2,6},{3,7},{4,8},{5,9},{6,10},{7,11},{8,12},{9,13},{1... | collective-permute-start | bytes 786440 | tf_op jit(solution)/shard_map/ppermute | solution.py:62
  14.0 1.5 %collective-permute-start.5 = (bf16[128,1024]{1,0:T(8,128)(2,1)}, bf16[128,1024]{1,0:T(8,128)(2,1)S(1)}, u32[]{:S(2)}, u32[]{:S(2)}) collective-permute-start(bf16[128,1024]{1,0:T(8,128)(2,1)} %param.1), channel_id=1, source_target_pairs={{0,12},{1,13},{2,14},{3,15},{4,0},{5,1},{6,2},{7,3},{8,4},{9,5},{1... | collective-permute-start | bytes 786440 | tf_op jit(solution)/shard_map/ppermute | solution.py:62
  15.5 1.0 %constant_dynamic-update-slice_fusion.5 = bf16[512,1024]{1,0:T(8,128)(2,1)S(1)} fusion(bf16[128,1024]{1,0:T(8,128)(2,1)} %param.1), kind=kLoop, calls=%fused_computation.8 | loop fusion | bytes 524288
  16.5 0.0 collective-permute-done
  16.6 0.3 collective-permute-done.1
  16.9 0.0 copy-start
  16.9 2.3 %collective-permute-start.2 = (bf16[256,1024]{1,0:T(8,128)(2,1)S(1)}, bf16[256,1024]{1,0:T(8,128)(2,1)S(1)}, u32[]{:S(2)}, u32[]{:S(2)}) collective-permute-start(bf16[256,1024]{1,0:T(8,128)(2,1)S(1)} %constant_dynamic-update-slice_fusion.refs_0_), channel_id=1, source_target_pairs={{0,32},{1,33},{2,34},{3,35},{4,36},{5,37},{6,38},{7,39},{8,40},{9,... | collective-permute-start | bytes 1572872 | tf_op jit(solution)/shard_map/ppermute | solution.py:62
  19.2 5.9 %collective-permute-start.3 = (bf16[256,1024]{1,0:T(8,128)(2,1)S(1)}, bf16[256,1024]{1,0:T(8,128)(2,1)S(1)}, u32[]{:S(2)}, u32[]{:S(2)}) collective-permute-start(bf16[256,1024]{1,0:T(8,128)(2,1)S(1)} %constant_dynamic-update-slice_fusion.refs_0_), channel_id=1, source_target_pairs={{0,96},{1,97},{2,98},{3,99},{4,100},{5,101},{6,102},{7,103},{8,104... | collective-permute-start | bytes 1572872 | tf_op jit(solution)/shard_map/ppermute | solution.py:62
  25.1 0.0 collective-permute-done.7
  25.1 0.0 collective-permute-start.8
  25.1 0.0 collective-permute-done.4
  25.1 2.7 %collective-permute-start.9 = (bf16[128,1024]{1,0:T(8,128)(2,1)S(1)}, bf16[128,1024]{1,0:T(8,128)(2,1)S(1)}, u32[]{:S(2)}, u32[]{:S(2)}) collective-permute-start(bf16[128,1024]{1,0:T(8,128)(2,1)S(1)} %collective-permute-done.7), channel_id=1, source_target_pairs={{0,12},{1,13},{2,14},{3,15},{4,0},{5,1},{6,2},{7,3},{8,4},{9,5},{1... | collective-permute-start | bytes 786440 | tf_op jit(solution)/shard_map/ppermute | solution.py:62
  27.8 0.0 collective-permute-done.5
  27.8 0.1 constant_dynamic-update-slice_fusion.3
  27.9 0.1 collective-permute-start.6
  28.0 6.6 %collective-permute-done.8 = bf16[128,1024]{1,0:T(8,128)(2,1)S(1)} collective-permute-done((bf16[128,1024]{1,0:T(8,128)(2,1)S(1)}, bf16[128,1024]{1,0:T(8,128)(2,1)S(1)}, u32[]{:S(2)}, u32[]{:S(2)}) %collective-permute-start.8) | collective-permute-done | bytes 262176 | tf_op jit(solution)/shard_map/ppermute | solution.py:62
  34.6 0.0 collective-permute-done.9
  34.6 0.1 pad_maximum_fusion.rows3
  34.7 0.0 copy-done
  34.7 0.7 %broadcast_select_fusion = bf16[128,1024]{1,0:T(8,128)(2,1)} fusion(bf16[128,1024]{1,0:T(8,128)(2,1)S(1)} %collective-permute-done.8, bf16[128,1024]{1,0:T(8,128)(2,1)S(1)} %collective-permute-done.9, pred[]{:T(512)S(6)} %eq.41), kind=kLoop, calls=%fused_computation.1 | loop fusion | flops 131072 | bytes 786433 | tf_op jit(solution)/shard_map/jit(_where)/select_n | solution.py:210
  35.4 0.9 %collective-permute-done.2.refs_0_ = bf16[256,1024]{1,0:T(8,128)(2,1)S(1)} collective-permute-done((bf16[256,1024]{1,0:T(8,128)(2,1)S(1)}, bf16[256,1024]{1,0:T(8,128)(2,1)S(1)}, u32[]{:S(2)}, u32[]{:S(2)}) %collective-permute-start.2) | collective-permute-done | bytes 524320 | tf_op jit(solution)/shard_map/ppermute | solution.py:62
  36.3 0.8 %slice.8 = bf16[128,1024]{1,0:T(8,128)(2,1)} slice(bf16[256,1024]{1,0:T(8,128)(2,1)S(1)} %collective-permute-done.2.refs_0_), slice={[0:128], [0:1024]} | slice | bytes 524288 | tf_op jit(solution)/shard_map/slice | solution.py:212
  37.1 0.0 collective-permute-done.3.refs_1_
  37.1 0.8 %slice.9 = bf16[128,1024]{1,0:T(8,128)(2,1)} slice(bf16[256,1024]{1,0:T(8,128)(2,1)S(1)} %collective-permute-done.3.refs_1_), slice={[128:256], [0:1024]} | slice | bytes 524288 | tf_op jit(solution)/shard_map/slice | solution.py:212
  37.9 0.0 collective-permute-done.6
  37.9 0.1 collective-permute-start.10
  38.0 0.5 collective-permute-start.14
  38.5 0.0 copy-done.2
  38.5 1.8 %collective-permute-start.11 = (bf16[128,1024]{1,0:T(8,128)(2,1)}, bf16[128,1024]{1,0:T(8,128)(2,1)S(1)}, u32[]{:S(2)}, u32[]{:S(2)}) collective-permute-start(bf16[128,1024]{1,0:T(8,128)(2,1)} %broadcast_select_fusion), channel_id=1, source_target_pairs={{0,4},{1,13},{2,6},{3,15},{4,8},{5,1},{6,10},{7,3},{8,12},{9,5},{1... | collective-permute-start | bytes 786440 | tf_op jit(solution)/shard_map/ppermute | solution.py:62
  40.3 0.0 copy-done.3
  40.3 0.0 collective-permute-start.12
  40.3 2.7 %collective-permute-start.13 = (bf16[128,1024]{1,0:T(8,128)(2,1)}, bf16[128,1024]{1,0:T(8,128)(2,1)}, u32[]{:S(2)}, u32[]{:S(2)}) collective-permute-start(bf16[128,1024]{1,0:T(8,128)(2,1)} %slice.9), channel_id=1, source_target_pairs={{0,96},{1,97},{2,98},{3,99},{4,100},{5,101},{6,102},{7,103},{8,104... | collective-permute-start | bytes 786440 | tf_op jit(solution)/shard_map/ppermute | solution.py:62
  43.0 0.1 stack.56.where
  43.1 0.0 collective-permute-done.10.swapped
  43.1 7.0 %own_rows_near.1 = (f32[2,4,2,2,128,1024]{5,4,3,2,1,0:T(8,128)}, bf16[512,1024]{1,0:T(8,128)(2,1)}, f32[8,512]{1,0:T(8,128)S(1)}) custom-call(s32[8]{0:T(128)S(1)} %stack.56.where, bf16[512,1024]{1,0:T(8,128)(2,1)S(1)} %constant_dynamic-update-slice_fusion.2.rows, bf16[512,1024]{1,0:T(8,128)(2,1)S(1)} %collective-permute-done.10.swapped, ...), custom_call_target="tpu_custom_call" | custom-call | flops 2147483648 | bytes 7340032 | tf_op jit(solution)/shard_map/own_rows_near/pallas_call | solution.py:124
  50.1 0.0 collective-permute-done.11.facing
  50.1 0.0 collective-permute-done.12.refs_1_
  50.1 0.0 collective-permute-done.13.refs_2_
  50.1 0.7 %copy-done.1 = bf16[128,1024]{1,0:T(8,128)(2,1)} copy-done((bf16[128,1024]{1,0:T(8,128)(2,1)}, bf16[128,1024]{1,0:T(8,128)(2,1)S(1)}, u32[]{:S(2)}) %copy-start.1) | copy-done | bytes 262168
  50.8 0.0 collective-permute-start.15
  50.8 0.1 stack.62.where
  50.9 6.6 %own_rows_far.1 = (f32[2,4,2,2,128,1024]{5,4,3,2,1,0:T(8,128)}, bf16[512,1024]{1,0:T(8,128)(2,1)S(1)}, f32[8,512]{1,0:T(8,128)S(1)}) custom-call(s32[8]{0:T(128)S(1)} %stack.62.where, bf16[512,1024]{1,0:T(8,128)(2,1)S(1)} %constant_dynamic-update-slice_fusion.2.rows, ...), custom_call_target="tpu_custom_call", output_to_operand_aliasing={{0}: (6, {})} | custom-call | flops 2147483648 | bytes 7340032 | tf_op jit(solution)/shard_map/own_rows_far/pallas_call | solution.py:124
  57.5 0.0 collective-permute-done.14.swapped3
  57.5 0.0 collective-permute-done.15.swapped_facing
  57.5 8.6 %across_rows.1 = f32[2,4,2,2,128,1024]{5,4,3,2,1,0:T(8,128)} custom-call(s32[8]{0:T(128)S(1)} %stack.56.where, bf16[384,1024]{1,0:T(8,128)(2,1)S(1)} %pad_maximum_fusion.rows3, bf16[128,1024]{1,0:T(8,128)(2,1)S(1)} %collective-permute-done.11.facing, bf16[384,1024]{1,0:T(8,128)(2,1)} %collective-permute-done.14.swapped3, ...), custom_call_target="tpu_custom_call", output_to_operand_aliasing={{}: (9, {})} | custom-call | flops 4294967296 | bytes 12582912 | tf_op jit(solution)/shard_map/across_rows/pallas_call | solution.py:162
  (7 shorter events, 0.1 us)
Async XLA Ops:
  0.0 16.6 %collective-permute-start = (bf16[128,1024]{1,0:T(8,128)(2,1)}, bf16[128,1024]{1,0:T(8,128)(2,1)S(1)}, u32[]{:S(2)}, u32[]{:S(2)}) collective-permute-start(bf16[128,1024]{1,0:T(8,128)(2,1)} %param.1), channel_id=1, source_target_pairs={{0,0},{1,64},{2,16},{3,80},{4,32},{5,96},{6,48},{7,112},{8,65},{9,... | collective-permute-start | bytes 786440 | tf_op jit(solution)/shard_map/ppermute | solution.py:62
  6.2 10.6 %collective-permute-start.1 = (bf16[128,1024]{1,0:T(8,128)(2,1)}, bf16[128,1024]{1,0:T(8,128)(2,1)S(1)}, u32[]{:S(2)}, u32[]{:S(2)}) collective-permute-start(bf16[128,1024]{1,0:T(8,128)(2,1)} %param.1), channel_id=1, source_target_pairs={{0,16},{1,80},{2,0},{3,64},{4,48},{5,112},{6,32},{7,96},{8,81},{9,... | collective-permute-start | bytes 786440 | tf_op jit(solution)/shard_map/ppermute | solution.py:62
  12.0 13.1 %collective-permute-start.7 = (bf16[128,1024]{1,0:T(8,128)(2,1)}, bf16[128,1024]{1,0:T(8,128)(2,1)S(1)}, u32[]{:S(2)}, u32[]{:S(2)}) collective-permute-start(bf16[128,1024]{1,0:T(8,128)(2,1)} %param.1), channel_id=1, source_target_pairs={{0,2},{1,3},{2,0},{3,1},{4,6},{5,7},{6,4},{7,5},{8,10},{9,11},{10,... | collective-permute-start | bytes 786440 | tf_op jit(solution)/shard_map/ppermute | solution.py:62
  12.9 12.3 %collective-permute-start.4 = (bf16[128,1024]{1,0:T(8,128)(2,1)}, bf16[128,1024]{1,0:T(8,128)(2,1)S(1)}, u32[]{:S(2)}, u32[]{:S(2)}) collective-permute-start(bf16[128,1024]{1,0:T(8,128)(2,1)} %param.1), channel_id=1, source_target_pairs={{0,4},{1,5},{2,6},{3,7},{4,8},{5,9},{6,10},{7,11},{8,12},{9,13},{1... | collective-permute-start | bytes 786440 | tf_op jit(solution)/shard_map/ppermute | solution.py:62
  14.0 13.8 %collective-permute-start.5 = (bf16[128,1024]{1,0:T(8,128)(2,1)}, bf16[128,1024]{1,0:T(8,128)(2,1)S(1)}, u32[]{:S(2)}, u32[]{:S(2)}) collective-permute-start(bf16[128,1024]{1,0:T(8,128)(2,1)} %param.1), channel_id=1, source_target_pairs={{0,12},{1,13},{2,14},{3,15},{4,0},{5,1},{6,2},{7,3},{8,4},{9,5},{1... | collective-permute-start | bytes 786440 | tf_op jit(solution)/shard_map/ppermute | solution.py:62
  16.9 17.8 %copy-start = (bf16[256,1024]{1,0:T(8,128)(2,1)}, bf16[256,1024]{1,0:T(8,128)(2,1)S(1)}, u32[]{:S(2)}) copy-start(bf16[256,1024]{1,0:T(8,128)(2,1)S(1)} %constant_dynamic-update-slice_fusion.refs_0_) | copy-start | bytes 1572868
  16.9 19.4 %collective-permute-start.2 = (bf16[256,1024]{1,0:T(8,128)(2,1)S(1)}, bf16[256,1024]{1,0:T(8,128)(2,1)S(1)}, u32[]{:S(2)}, u32[]{:S(2)}) collective-permute-start(bf16[256,1024]{1,0:T(8,128)(2,1)S(1)} %constant_dynamic-update-slice_fusion.refs_0_), channel_id=1, source_target_pairs={{0,32},{1,33},{2,34},{3,35},{4,36},{5,37},{6,38},{7,39},{8,40},{9,... | collective-permute-start | bytes 1572872 | tf_op jit(solution)/shard_map/ppermute | solution.py:62
  19.2 17.9 %collective-permute-start.3 = (bf16[256,1024]{1,0:T(8,128)(2,1)S(1)}, bf16[256,1024]{1,0:T(8,128)(2,1)S(1)}, u32[]{:S(2)}, u32[]{:S(2)}) collective-permute-start(bf16[256,1024]{1,0:T(8,128)(2,1)S(1)} %constant_dynamic-update-slice_fusion.refs_0_), channel_id=1, source_target_pairs={{0,96},{1,97},{2,98},{3,99},{4,100},{5,101},{6,102},{7,103},{8,104... | collective-permute-start | bytes 1572872 | tf_op jit(solution)/shard_map/ppermute | solution.py:62
  25.1 9.5 %collective-permute-start.8 = (bf16[128,1024]{1,0:T(8,128)(2,1)S(1)}, bf16[128,1024]{1,0:T(8,128)(2,1)S(1)}, u32[]{:S(2)}, u32[]{:S(2)}) collective-permute-start(bf16[128,1024]{1,0:T(8,128)(2,1)S(1)} %collective-permute-done.7), channel_id=1, source_target_pairs={{0,4},{1,5},{2,6},{3,7},{4,8},{5,9},{6,10},{7,11},{8,12},{9,13},{1... | collective-permute-start | bytes 786440 | tf_op jit(solution)/shard_map/ppermute | solution.py:62
  25.1 9.5 %collective-permute-start.9 = (bf16[128,1024]{1,0:T(8,128)(2,1)S(1)}, bf16[128,1024]{1,0:T(8,128)(2,1)S(1)}, u32[]{:S(2)}, u32[]{:S(2)}) collective-permute-start(bf16[128,1024]{1,0:T(8,128)(2,1)S(1)} %collective-permute-done.7), channel_id=1, source_target_pairs={{0,12},{1,13},{2,14},{3,15},{4,0},{5,1},{6,2},{7,3},{8,4},{9,5},{1... | collective-permute-start | bytes 786440 | tf_op jit(solution)/shard_map/ppermute | solution.py:62
  27.9 9.9 %collective-permute-start.6 = (bf16[128,1024]{1,0:T(8,128)(2,1)S(1)}, bf16[128,1024]{1,0:T(8,128)(2,1)S(1)}, u32[]{:S(2)}, u32[]{:S(2)}) collective-permute-start(bf16[128,1024]{1,0:T(8,128)(2,1)S(1)} %get-tuple-element.44), channel_id=1, source_target_pairs={{0,4},{1,13},{2,6},{3,15},{4,8},{5,1},{6,10},{7,3},{8,12},{9,5},{1... | collective-permute-start | bytes 786440 | tf_op jit(solution)/shard_map/ppermute | solution.py:62
  36.3 2.2 %copy-start.2 = (bf16[256,1024]{1,0:T(8,128)(2,1)}, bf16[256,1024]{1,0:T(8,128)(2,1)S(1)}, u32[]{:S(2)}) copy-start(bf16[256,1024]{1,0:T(8,128)(2,1)S(1)} %collective-permute-done.2.refs_0_) | copy-start | bytes 1572868
  37.1 3.2 %copy-start.3 = (bf16[256,1024]{1,0:T(8,128)(2,1)}, bf16[256,1024]{1,0:T(8,128)(2,1)S(1)}, u32[]{:S(2)}) copy-start(bf16[256,1024]{1,0:T(8,128)(2,1)S(1)} %collective-permute-done.3.refs_1_) | copy-start | bytes 1572868
  37.9 5.2 %collective-permute-start.10 = (bf16[512,1024]{1,0:T(8,128)(2,1)S(1)}, bf16[512,1024]{1,0:T(8,128)(2,1)S(1)}, u32[]{:S(2)}, u32[]{:S(2)}) collective-permute-start(bf16[512,1024]{1,0:T(8,128)(2,1)S(1)} %constant_dynamic-update-slice_fusion.2.rows), channel_id=1, source_target_pairs={{0,1},{1,0},{2,3},{3,2},{4,5},{5,4},{6,7},{7,6},{8,9},{9,8},{10,11... | collective-permute-start | bytes 3145736 | tf_op jit(solution)/shard_map/ppermute | solution.py:62
  38.0 19.5 %collective-permute-start.14 = (bf16[384,1024]{1,0:T(8,128)(2,1)S(1)}, bf16[384,1024]{1,0:T(8,128)(2,1)}, u32[]{:S(2)}, u32[]{:S(2)}) collective-permute-start(bf16[384,1024]{1,0:T(8,128)(2,1)S(1)} %pad_maximum_fusion.rows3), channel_id=1, source_target_pairs={{0,1},{1,0},{2,3},{3,2},{4,5},{5,4},{6,7},{7,6},{8,9},{9,8},{10,11... | collective-permute-start | bytes 2359304 | tf_op jit(solution)/shard_map/ppermute | solution.py:62
  38.5 11.6 %collective-permute-start.11 = (bf16[128,1024]{1,0:T(8,128)(2,1)}, bf16[128,1024]{1,0:T(8,128)(2,1)S(1)}, u32[]{:S(2)}, u32[]{:S(2)}) collective-permute-start(bf16[128,1024]{1,0:T(8,128)(2,1)} %broadcast_select_fusion), channel_id=1, source_target_pairs={{0,4},{1,13},{2,6},{3,15},{4,8},{5,1},{6,10},{7,3},{8,12},{9,5},{1... | collective-permute-start | bytes 786440 | tf_op jit(solution)/shard_map/ppermute | solution.py:62
  40.3 9.8 %collective-permute-start.12 = (bf16[128,1024]{1,0:T(8,128)(2,1)}, bf16[128,1024]{1,0:T(8,128)(2,1)S(1)}, u32[]{:S(2)}, u32[]{:S(2)}) collective-permute-start(bf16[128,1024]{1,0:T(8,128)(2,1)} %slice.8), channel_id=1, source_target_pairs={{0,32},{1,33},{2,34},{3,35},{4,36},{5,37},{6,38},{7,39},{8,40},{9,... | collective-permute-start | bytes 786440 | tf_op jit(solution)/shard_map/ppermute | solution.py:62
  40.3 9.8 %collective-permute-start.13 = (bf16[128,1024]{1,0:T(8,128)(2,1)}, bf16[128,1024]{1,0:T(8,128)(2,1)}, u32[]{:S(2)}, u32[]{:S(2)}) collective-permute-start(bf16[128,1024]{1,0:T(8,128)(2,1)} %slice.9), channel_id=1, source_target_pairs={{0,96},{1,97},{2,98},{3,99},{4,100},{5,101},{6,102},{7,103},{8,104... | collective-permute-start | bytes 786440 | tf_op jit(solution)/shard_map/ppermute | solution.py:62
  50.1 0.7 %copy-start.1 = (bf16[128,1024]{1,0:T(8,128)(2,1)}, bf16[128,1024]{1,0:T(8,128)(2,1)S(1)}, u32[]{:S(2)}) copy-start(bf16[128,1024]{1,0:T(8,128)(2,1)S(1)} %collective-permute-done.12.refs_1_) | copy-start | bytes 786436
  50.8 6.7 %collective-permute-start.15 = (bf16[128,1024]{1,0:T(8,128)(2,1)S(1)}, bf16[128,1024]{1,0:T(8,128)(2,1)S(1)}, u32[]{:S(2)}, u32[]{:S(2)}) collective-permute-start(bf16[128,1024]{1,0:T(8,128)(2,1)S(1)} %collective-permute-done.11.facing), channel_id=1, source_target_pairs={{0,1},{1,0},{2,3},{3,2},{4,5},{5,4},{6,7},{7,6},{8,9},{9,8},{10,11... | collective-permute-start | bytes 786440 | tf_op jit(solution)/shard_map/ppermute | solution.py:62

commit v4 on v3

--- a/solution.py
+++ b/solution.py
@@ -38,7 +38,7 @@
 Y_DOWN = moves(lambda x, y, z, c: (x, (y + 3) % 4, z, c))
 Z_UP = moves(lambda x, y, z, c: (x, y, (z + 1) % 4, c))
 Z_DOWN = moves(lambda x, y, z, c: (x, y, (z + 3) % 4, c))
-Z_SPLIT_CROSS = moves(lambda x, y, z, c: (x, y, (z + 1 + 2 * c) % 4, 1 - c))
+Y_SPLIT = moves(lambda x, y, z, c: (x, (y + 1 + 2 * c) % 4, z, c))
 Z_SPLIT = moves(lambda x, y, z, c: (x, y, (z + 1 + 2 * c) % 4, c))
 
 
@@ -82,8 +82,9 @@
         for part, lhs in enumerate((a, turned)):
             cross = lax.dot_general(lhs, b[...], NT, preferred_element_type=F32)
             scaled = cross * row_inv * col_inv[0:1, :]
-            out[part, 0, 0, core, :, at] = scaled[:SHARD]
-            out[part, 0, 0, 1 - core, :, at] = scaled[SHARD:]
+            n = rows.shape[0] // SHARD
+            out[part, :, 0, core, :, at] = scaled[: n * SHARD].reshape(n, SHARD, -1)
+            out[part, :, 0, 1 - core, :, at] = scaled[n * SHARD :].reshape(n, SHARD, -1)
 
 
 def half_kernel(where, rows, swapped, *refs):
@@ -107,15 +108,13 @@
     return lax.rem(where[0] + jnp.where(step == 1, 3, jnp.where(step == 2, 1, jnp.where(step == 3, 2, 0))), 4)
 
 
-SHARD_SPEC = pl.BlockSpec((SHARD, SPEC), lambda step, where: (step, 0))
-
-
 def half_call(where, rows, swapped, pieces, before, name):
     def place_out(step, where):
-        return 0, z_of(step, where), where[1], 0, 0, where[3]
-
+        return 0, step, where[1], 0, 0, where[3]
+
+    pair = pl.BlockSpec((TILE, SPEC), lambda step, where: (step, 0))
     vmem, anywhere = pl.BlockSpec(memory_space=pltpu.VMEM), pl.BlockSpec(memory_space=pl.ANY)
-    in_specs = [SHARD_SPEC, SHARD_SPEC] + [anywhere] * len(pieces)
+    in_specs = [pair, pair] + [anywhere] * len(pieces)
     operands, aliases = (rows, swapped, *[in_hbm(piece) for piece in pieces]), {}
     if before is not None:
         aliases = {1 + len(operands): 0}
@@ -125,9 +124,9 @@
         half_kernel,
         grid_spec=pltpu.PrefetchScalarGridSpec(
             num_scalar_prefetch=1,
-            grid=(4,),
+            grid=(2,),
             in_specs=in_specs,
-            out_specs=[pl.BlockSpec((2, 1, 1, 2, SHARD, WIDE), place_out), vmem, vmem],
+            out_specs=[pl.BlockSpec((2, 2, 1, 2, SHARD, WIDE), place_out), vmem, vmem],
             scratch_shapes=[pltpu.SemaphoreType.DMA((4,))],
         ),
         out_shape=[
@@ -191,6 +190,13 @@
     return jnp.concatenate(shards, axis=0)
 
 
+def by_z(z, own, below, above, facing):
+    rows = jnp.zeros((4 * SHARD, SPEC), BF16)
+    for shard, up in ((own, 0), (below, 3), (above, 1), (facing, 2)):
+        rows = lax.dynamic_update_slice(rows, shard, ((z + up) % 4 * SHARD, 0))
+    return rows
+
+
 def shards(x):
     row, col = lax.axis_index("row"), lax.axis_index("col")
     low, y, z, high, core = row % 2, row // 2, col // 4, col // 2 % 2, col % 2
@@ -209,16 +215,16 @@
     below_across, above_across = send(across, Z_UP), send(across, Z_DOWN)
     onward = jnp.where(core == 0, below_across, above_across)
     rows_across = family(across, below_across, above_across)
-    up, down, facing, rows_across, onward, up_a, down_b = together(up, down, facing, rows_across, onward, up[:SHARD], down[SHARD:])
-    far0, far1 = send(up_a, Y_UP), send(down_b, Y_DOWN)
-    rows = family(x, below, above, facing)
+    up, down, facing, rows_across, onward, far = together(up, down, facing, rows_across, onward, jnp.where(core == 0, up, down))
+    far = send(far, Y_SPLIT)
+    rows = by_z(z, x, below, above, facing)
     swapped = send(rows, SWAP_CORE)
     facing_across = send(onward, Z_SPLIT)
     out, *first = half_call(where, rows, swapped, (up, down), None, "own_rows_near")
-    out, facing_across, far0, far1 = together(out, facing_across, far0, far1)
+    out, facing_across, far = together(out, facing_across, far)
     swapped_across = send(rows_across, SWAP_CORE)
     facing_swapped = send(facing_across, SWAP_CORE)
-    out, *second = half_call(where_far, rows, swapped, (own, far0, far1), out, "own_rows_far")
+    out, *second = half_call(where_far, rows, swapped, (own, far), out, "own_rows_far")
     out = last_call(where, (rows_across, facing_across, swapped_across, facing_swapped), first, second, out)
     return out.reshape(2, 4 * 4 * SHARD, COLS)
 

time: 66.3 us -> 63.3 us (0.955)
  local copies, waits for them, and re-layouts: 3.48 us -> 1.35 us
  starting transfers between devices: 31.6 us -> 30.7 us
    unnamed x11 -> x7, local copies, waits for them, and re-layouts: 1.73 us -> 0.03 us
    slice x2 -> x0, local copies, waits for them, and re-layouts: 1.55 us -> none  [the longest x1 0.78 us: shards(): up[:SHARD]]
    dynamic_update_slice x0 -> x3, local copies, waits for them, and re-layouts: none -> 1.02 us  [by_z(): rows = lax.dynamic_update_slice(rows, shard, ((z + up) % 4 * SHARD, 0))]
    select_n x0 -> x1, other arithmetic: none -> 0.94 us  [shards(): jnp.where(core == 0, up, down)]
    ppermute x16 -> x15, starting transfers between devices: 31.6 us -> 30.7 us  [send(): return lax.ppermute(value, AXES, pairs)]
    select_n x1, other arithmetic: 0.72 us -> 0.03 us  [shards(): onward = jnp.where(core == 0, below_across, above_across)]
    ppermute x16 -> x15, waiting for transfers between devices: 7.83 us -> 7.9 us  [send(): return lax.ppermute(value, AXES, pairs)]
  transfers between devices with their start and end apart: 16 -> 15, of which waited for: 3 -> 3; matrix products, arithmetic and copies ran while one was open for 5% -> 4% of each run, Pallas kernels for 21% -> 20%
where the time goes in v4:
time: 63.3 us; the launch traced here: 63.1 us
  starting transfers between devices  30.7 us (48%)
  Pallas kernels  21.5 us (34%)
  waiting for transfers between devices  7.9 us (12%)
  local copies, waits for them, and re-layouts  1.35 us (2%)
  other arithmetic  1.1 us (2%)
    ppermute x15, starting transfers between devices, send(): return lax.ppermute(value, AXES, pairs)  30.7 us
    pallas_call x2, Pallas kernels, half_call(): pl.pallas_call(half_kernel, grid_spec=pltpu.PrefetchScalarGridSpec(num_sc...  12.9 us
    pallas_call x1, Pallas kernels, last_call(): pl.pallas_call(last_kernel, grid_spec=pltpu.PrefetchScalarGridSpec(num_sc...  8.6 us
    ppermute x15, waiting for transfers between devices, send(): return lax.ppermute(value, AXES, pairs)  7.9 us
  transfers between devices with their start and end apart: 15, of which 3 were waited for; matrix products, arithmetic and copies ran while one was open for 4% of the time, Pallas kernels for 20%

profile of v4, /device:TPU:1, one launch (start us, length us, event | category | flops | bytes accessed | tf_op | source)
XLA Modules:
  0.0 63.1 jit_solution(679672845501773651)
XLA Ops:
  0.0 6.2 %collective-permute-start = (bf16[128,1024]{1,0:T(8,128)(2,1)}, bf16[128,1024]{1,0:T(8,128)(2,1)S(1)}, u32[]{:S(2)}, u32[]{:S(2)}) collective-permute-start(bf16[128,1024]{1,0:T(8,128)(2,1)} %param.1), channel_id=1, source_target_pairs={{0,0},{1,64},{2,16},{3,80},{4,32},{5,96},{6,48},{7,112},{8,65},{9,... | collective-permute-start | bytes 786440 | tf_op jit(solution)/shard_map/ppermute | solution.py:62
  6.2 5.8 %collective-permute-start.1 = (bf16[128,1024]{1,0:T(8,128)(2,1)}, bf16[128,1024]{1,0:T(8,128)(2,1)S(1)}, u32[]{:S(2)}, u32[]{:S(2)}) collective-permute-start(bf16[128,1024]{1,0:T(8,128)(2,1)} %param.1), channel_id=1, source_target_pairs={{0,16},{1,80},{2,0},{3,64},{4,48},{5,112},{6,32},{7,96},{8,81},{9,... | collective-permute-start | bytes 786440 | tf_op jit(solution)/shard_map/ppermute | solution.py:62
  12.0 1.2 %collective-permute-start.4 = (bf16[128,1024]{1,0:T(8,128)(2,1)}, bf16[128,1024]{1,0:T(8,128)(2,1)S(1)}, u32[]{:S(2)}, u32[]{:S(2)}) collective-permute-start(bf16[128,1024]{1,0:T(8,128)(2,1)} %param.1), channel_id=1, source_target_pairs={{0,4},{1,5},{2,6},{3,7},{4,8},{5,9},{6,10},{7,11},{8,12},{9,13},{1... | collective-permute-start | bytes 786440 | tf_op jit(solution)/shard_map/ppermute | solution.py:62
  13.2 1.5 %collective-permute-start.5 = (bf16[128,1024]{1,0:T(8,128)(2,1)}, bf16[128,1024]{1,0:T(8,128)(2,1)S(1)}, u32[]{:S(2)}, u32[]{:S(2)}) collective-permute-start(bf16[128,1024]{1,0:T(8,128)(2,1)} %param.1), channel_id=1, source_target_pairs={{0,12},{1,13},{2,14},{3,15},{4,0},{5,1},{6,2},{7,3},{8,4},{9,5},{1... | collective-permute-start | bytes 786440 | tf_op jit(solution)/shard_map/ppermute | solution.py:62
  14.7 0.8 %collective-permute-start.7 = (bf16[128,1024]{1,0:T(8,128)(2,1)}, bf16[128,1024]{1,0:T(8,128)(2,1)S(1)}, u32[]{:S(2)}, u32[]{:S(2)}) collective-permute-start(bf16[128,1024]{1,0:T(8,128)(2,1)} %param.1), channel_id=1, source_target_pairs={{0,2},{1,3},{2,0},{3,1},{4,6},{5,7},{6,4},{7,5},{8,10},{9,11},{10,... | collective-permute-start | bytes 786440 | tf_op jit(solution)/shard_map/ppermute | solution.py:62
  15.5 0.1 broadcast_in_dim.3
  15.7 1.0 %constant_dynamic-update-slice_fusion.5 = bf16[512,1024]{1,0:T(8,128)(2,1)S(1)} fusion(bf16[512,1024]{1,0:T(8,128)(2,1)S(1)} %broadcast_in_dim.3, bf16[128,1024]{1,0:T(8,128)(2,1)} %param.1, s32[]{:T(128)S(6)} %select_n.222), kind=kLoop, calls=%fused_computation.9 | loop fusion | bytes 524292 | tf_op jit(solution)/shard_map/dynamic_update_slice | solution.py:196
  16.7 0.0 collective-permute-done
  16.7 0.0 collective-permute-done.1
  16.8 0.0 copy-start
  16.8 2.1 %collective-permute-start.2 = (bf16[256,1024]{1,0:T(8,128)(2,1)S(1)}, bf16[256,1024]{1,0:T(8,128)(2,1)S(1)}, u32[]{:S(2)}, u32[]{:S(2)}) collective-permute-start(bf16[256,1024]{1,0:T(8,128)(2,1)S(1)} %constant_dynamic-update-slice_fusion.refs_0_), channel_id=1, source_target_pairs={{0,32},{1,33},{2,34},{3,35},{4,36},{5,37},{6,38},{7,39},{8,40},{9,... | collective-permute-start | bytes 1572872 | tf_op jit(solution)/shard_map/ppermute | solution.py:62
  18.9 4.9 %collective-permute-start.3 = (bf16[256,1024]{1,0:T(8,128)(2,1)S(1)}, bf16[256,1024]{1,0:T(8,128)(2,1)S(1)}, u32[]{:S(2)}, u32[]{:S(2)}) collective-permute-start(bf16[256,1024]{1,0:T(8,128)(2,1)S(1)} %constant_dynamic-update-slice_fusion.refs_0_), channel_id=1, source_target_pairs={{0,96},{1,97},{2,98},{3,99},{4,100},{5,101},{6,102},{7,103},{8,104... | collective-permute-start | bytes 1572872 | tf_op jit(solution)/shard_map/ppermute | solution.py:62
  23.7 0.0 collective-permute-done.7
  23.7 0.7 %collective-permute-start.8 = (bf16[128,1024]{1,0:T(8,128)(2,1)S(1)}, bf16[128,1024]{1,0:T(8,128)(2,1)S(1)}, u32[]{:S(2)}, u32[]{:S(2)}) collective-permute-start(bf16[128,1024]{1,0:T(8,128)(2,1)S(1)} %collective-permute-done.7), channel_id=1, source_target_pairs={{0,4},{1,5},{2,6},{3,7},{4,8},{5,9},{6,10},{7,11},{8,12},{9,13},{1... | collective-permute-start | bytes 786440 | tf_op jit(solution)/shard_map/ppermute | solution.py:62
  24.4 0.0 collective-permute-done.4
  24.4 2.0 %collective-permute-start.9 = (bf16[128,1024]{1,0:T(8,128)(2,1)S(1)}, bf16[128,1024]{1,0:T(8,128)(2,1)S(1)}, u32[]{:S(2)}, u32[]{:S(2)}) collective-permute-start(bf16[128,1024]{1,0:T(8,128)(2,1)S(1)} %collective-permute-done.7), channel_id=1, source_target_pairs={{0,12},{1,13},{2,14},{3,15},{4,0},{5,1},{6,2},{7,3},{8,4},{9,5},{1... | collective-permute-start | bytes 786440 | tf_op jit(solution)/shard_map/ppermute | solution.py:62
  26.5 0.0 collective-permute-done.5
  26.5 0.1 constant_dynamic-update-slice_fusion.3
  26.5 0.1 collective-permute-start.6
  26.6 4.7 %collective-permute-done.8 = bf16[128,1024]{1,0:T(8,128)(2,1)S(1)} collective-permute-done((bf16[128,1024]{1,0:T(8,128)(2,1)S(1)}, bf16[128,1024]{1,0:T(8,128)(2,1)S(1)}, u32[]{:S(2)}, u32[]{:S(2)}) %collective-permute-start.8) | collective-permute-done | bytes 262176 | tf_op jit(solution)/shard_map/ppermute | solution.py:62
  31.4 0.0 collective-permute-done.9
  31.4 0.1 pad_maximum_fusion.rows3
  31.4 0.0 copy-done
  31.5 2.2 %collective-permute-done.2.refs_0_ = bf16[256,1024]{1,0:T(8,128)(2,1)S(1)} collective-permute-done((bf16[256,1024]{1,0:T(8,128)(2,1)S(1)}, bf16[256,1024]{1,0:T(8,128)(2,1)S(1)}, u32[]{:S(2)}, u32[]{:S(2)}) %collective-permute-start.2) | collective-permute-done | bytes 524320 | tf_op jit(solution)/shard_map/ppermute | solution.py:62
  33.7 0.0 copy-start.1
  33.7 0.0 collective-permute-done.3.refs_1_
  33.7 0.0 copy-start.2
  33.7 0.9 %broadcast_select_fusion = bf16[256,1024]{1,0:T(8,128)(2,1)} fusion(bf16[256,1024]{1,0:T(8,128)(2,1)S(1)} %collective-permute-done.2.refs_0_, bf16[256,1024]{1,0:T(8,128)(2,1)S(1)} %collective-permute-done.3.refs_1_, pred[]{:T(512)S(6)} %eq.46), kind=kLoop, calls=%fused_computation.1 | loop fusion | flops 262144 | bytes 1572865 | tf_op jit(solution)/shard_map/jit(_where)/select_n | solution.py:218
  34.6 0.9 %collective-permute-done.6 = bf16[128,1024]{1,0:T(8,128)(2,1)S(1)} collective-permute-done((bf16[128,1024]{1,0:T(8,128)(2,1)S(1)}, bf16[128,1024]{1,0:T(8,128)(2,1)S(1)}, u32[]{:S(2)}, u32[]{:S(2)}) %collective-permute-start.6) | collective-permute-done | bytes 262176 | tf_op jit(solution)/shard_map/ppermute | solution.py:62
  35.6 1.0 %collective-permute-start.10 = (bf16[512,1024]{1,0:T(8,128)(2,1)S(1)}, bf16[512,1024]{1,0:T(8,128)(2,1)S(1)}, u32[]{:S(2)}, u32[]{:S(2)}) collective-permute-start(bf16[512,1024]{1,0:T(8,128)(2,1)S(1)} %constant_dynamic-update-slice_fusion.2.rows), channel_id=1, source_target_pairs={{0,1},{1,0},{2,3},{3,2},{4,5},{5,4},{6,7},{7,6},{8,9},{9,8},{10,11... | collective-permute-start | bytes 3145736 | tf_op jit(solution)/shard_map/ppermute | solution.py:62
  36.6 2.0 %collective-permute-start.12 = (bf16[256,1024]{1,0:T(8,128)(2,1)}, bf16[256,1024]{1,0:T(8,128)(2,1)}, u32[]{:S(2)}, u32[]{:S(2)}) collective-permute-start(bf16[256,1024]{1,0:T(8,128)(2,1)} %broadcast_select_fusion), channel_id=1, source_target_pairs={{0,32},{1,97},{2,34},{3,99},{4,36},{5,101},{6,38},{7,103},{8,40},{... | collective-permute-start | bytes 1572872 | tf_op jit(solution)/shard_map/ppermute | solution.py:62
  38.6 0.0 copy-done.1
  38.6 0.0 collective-permute-start.13
  38.7 0.0 copy-done.2
  38.7 2.4 %collective-permute-start.11 = (bf16[128,1024]{1,0:T(8,128)(2,1)S(1)}, bf16[128,1024]{1,0:T(8,128)(2,1)S(1)}, u32[]{:S(2)}, u32[]{:S(2)}) collective-permute-start(bf16[128,1024]{1,0:T(8,128)(2,1)S(1)} %broadcast_select_fusion.1), channel_id=1, source_target_pairs={{0,4},{1,13},{2,6},{3,15},{4,8},{5,1},{6,10},{7,3},{8,12},{9,5},{1... | collective-permute-start | bytes 786440 | tf_op jit(solution)/shard_map/ppermute | solution.py:62
  41.0 0.1 stack.56.where
  41.1 0.0 collective-permute-done.10.swapped
  41.1 6.6 %own_rows_near.1 = (f32[2,4,2,2,128,1024]{5,4,3,2,1,0:T(8,128)}, bf16[512,1024]{1,0:T(8,128)(2,1)}, f32[8,512]{1,0:T(8,128)S(1)}) custom-call(s32[8]{0:T(128)S(1)} %stack.56.where, bf16[512,1024]{1,0:T(8,128)(2,1)S(1)} %constant_dynamic-update-slice_fusion.2.rows, bf16[512,1024]{1,0:T(8,128)(2,1)S(1)} %collective-permute-done.10.swapped, ...), custom_call_target="tpu_custom_call" | custom-call | flops 2147483648 | bytes 7340032 | tf_op jit(solution)/shard_map/own_rows_near/pallas_call | solution.py:123
  47.8 0.0 collective-permute-done.11.facing
  47.8 0.0 collective-permute-done.12.refs_1_
  47.8 0.1 collective-permute-start.14
  48.1 0.1 stack.62.where
  48.2 6.3 %own_rows_far.1 = (f32[2,4,2,2,128,1024]{5,4,3,2,1,0:T(8,128)}, bf16[512,1024]{1,0:T(8,128)(2,1)S(1)}, f32[8,512]{1,0:T(8,128)S(1)}) custom-call(s32[8]{0:T(128)S(1)} %stack.62.where, bf16[512,1024]{1,0:T(8,128)(2,1)S(1)} %constant_dynamic-update-slice_fusion.2.rows, ...), custom_call_target="tpu_custom_call", output_to_operand_aliasing={{0}: (5, {})} | custom-call | flops 2147483648 | bytes 7340032 | tf_op jit(solution)/shard_map/own_rows_far/pallas_call | solution.py:123
  54.5 0.0 collective-permute-done.13.swapped3
  54.5 0.0 collective-permute-done.14.swapped_facing
  54.5 8.6 %across_rows.1 = f32[2,4,2,2,128,1024]{5,4,3,2,1,0:T(8,128)} custom-call(s32[8]{0:T(128)S(1)} %stack.56.where, bf16[384,1024]{1,0:T(8,128)(2,1)S(1)} %pad_maximum_fusion.rows3, bf16[128,1024]{1,0:T(8,128)(2,1)S(1)} %collective-permute-done.11.facing, bf16[384,1024]{1,0:T(8,128)(2,1)} %collective-permute-done.13.swapped3, ...), custom_call_target="tpu_custom_call", output_to_operand_aliasing={{}: (9, {})} | custom-call | flops 4294967296 | bytes 12582912 | tf_op jit(solution)/shard_map/across_rows/pallas_call | solution.py:161
  (5 shorter events, 0.1 us)
Async XLA Ops:
  0.0 16.7 %collective-permute-start = (bf16[128,1024]{1,0:T(8,128)(2,1)}, bf16[128,1024]{1,0:T(8,128)(2,1)S(1)}, u32[]{:S(2)}, u32[]{:S(2)}) collective-permute-start(bf16[128,1024]{1,0:T(8,128)(2,1)} %param.1), channel_id=1, source_target_pairs={{0,0},{1,64},{2,16},{3,80},{4,32},{5,96},{6,48},{7,112},{8,65},{9,... | collective-permute-start | bytes 786440 | tf_op jit(solution)/shard_map/ppermute | solution.py:62
  6.2 10.5 %collective-permute-start.1 = (bf16[128,1024]{1,0:T(8,128)(2,1)}, bf16[128,1024]{1,0:T(8,128)(2,1)S(1)}, u32[]{:S(2)}, u32[]{:S(2)}) collective-permute-start(bf16[128,1024]{1,0:T(8,128)(2,1)} %param.1), channel_id=1, source_target_pairs={{0,16},{1,80},{2,0},{3,64},{4,48},{5,112},{6,32},{7,96},{8,81},{9,... | collective-permute-start | bytes 786440 | tf_op jit(solution)/shard_map/ppermute | solution.py:62
  12.0 12.4 %collective-permute-start.4 = (bf16[128,1024]{1,0:T(8,128)(2,1)}, bf16[128,1024]{1,0:T(8,128)(2,1)S(1)}, u32[]{:S(2)}, u32[]{:S(2)}) collective-permute-start(bf16[128,1024]{1,0:T(8,128)(2,1)} %param.1), channel_id=1, source_target_pairs={{0,4},{1,5},{2,6},{3,7},{4,8},{5,9},{6,10},{7,11},{8,12},{9,13},{1... | collective-permute-start | bytes 786440 | tf_op jit(solution)/shard_map/ppermute | solution.py:62
  13.2 13.3 %collective-permute-start.5 = (bf16[128,1024]{1,0:T(8,128)(2,1)}, bf16[128,1024]{1,0:T(8,128)(2,1)S(1)}, u32[]{:S(2)}, u32[]{:S(2)}) collective-permute-start(bf16[128,1024]{1,0:T(8,128)(2,1)} %param.1), channel_id=1, source_target_pairs={{0,12},{1,13},{2,14},{3,15},{4,0},{5,1},{6,2},{7,3},{8,4},{9,5},{1... | collective-permute-start | bytes 786440 | tf_op jit(solution)/shard_map/ppermute | solution.py:62
  14.7 9.1 %collective-permute-start.7 = (bf16[128,1024]{1,0:T(8,128)(2,1)}, bf16[128,1024]{1,0:T(8,128)(2,1)S(1)}, u32[]{:S(2)}, u32[]{:S(2)}) collective-permute-start(bf16[128,1024]{1,0:T(8,128)(2,1)} %param.1), channel_id=1, source_target_pairs={{0,2},{1,3},{2,0},{3,1},{4,6},{5,7},{6,4},{7,5},{8,10},{9,11},{10,... | collective-permute-start | bytes 786440 | tf_op jit(solution)/shard_map/ppermute | solution.py:62
  16.8 14.6 %copy-start = (bf16[256,1024]{1,0:T(8,128)(2,1)}, bf16[256,1024]{1,0:T(8,128)(2,1)S(1)}, u32[]{:S(2)}) copy-start(bf16[256,1024]{1,0:T(8,128)(2,1)S(1)} %constant_dynamic-update-slice_fusion.refs_0_) | copy-start | bytes 1572868
  16.8 16.9 %collective-permute-start.2 = (bf16[256,1024]{1,0:T(8,128)(2,1)S(1)}, bf16[256,1024]{1,0:T(8,128)(2,1)S(1)}, u32[]{:S(2)}, u32[]{:S(2)}) collective-permute-start(bf16[256,1024]{1,0:T(8,128)(2,1)S(1)} %constant_dynamic-update-slice_fusion.refs_0_), channel_id=1, source_target_pairs={{0,32},{1,33},{2,34},{3,35},{4,36},{5,37},{6,38},{7,39},{8,40},{9,... | collective-permute-start | bytes 1572872 | tf_op jit(solution)/shard_map/ppermute | solution.py:62
  18.9 14.8 %collective-permute-start.3 = (bf16[256,1024]{1,0:T(8,128)(2,1)S(1)}, bf16[256,1024]{1,0:T(8,128)(2,1)S(1)}, u32[]{:S(2)}, u32[]{:S(2)}) collective-permute-start(bf16[256,1024]{1,0:T(8,128)(2,1)S(1)} %constant_dynamic-update-slice_fusion.refs_0_), channel_id=1, source_target_pairs={{0,96},{1,97},{2,98},{3,99},{4,100},{5,101},{6,102},{7,103},{8,104... | collective-permute-start | bytes 1572872 | tf_op jit(solution)/shard_map/ppermute | solution.py:62
  23.7 7.6 %collective-permute-start.8 = (bf16[128,1024]{1,0:T(8,128)(2,1)S(1)}, bf16[128,1024]{1,0:T(8,128)(2,1)S(1)}, u32[]{:S(2)}, u32[]{:S(2)}) collective-permute-start(bf16[128,1024]{1,0:T(8,128)(2,1)S(1)} %collective-permute-done.7), channel_id=1, source_target_pairs={{0,4},{1,5},{2,6},{3,7},{4,8},{5,9},{6,10},{7,11},{8,12},{9,13},{1... | collective-permute-start | bytes 786440 | tf_op jit(solution)/shard_map/ppermute | solution.py:62
  24.4 7.0 %collective-permute-start.9 = (bf16[128,1024]{1,0:T(8,128)(2,1)S(1)}, bf16[128,1024]{1,0:T(8,128)(2,1)S(1)}, u32[]{:S(2)}, u32[]{:S(2)}) collective-permute-start(bf16[128,1024]{1,0:T(8,128)(2,1)S(1)} %collective-permute-done.7), channel_id=1, source_target_pairs={{0,12},{1,13},{2,14},{3,15},{4,0},{5,1},{6,2},{7,3},{8,4},{9,5},{1... | collective-permute-start | bytes 786440 | tf_op jit(solution)/shard_map/ppermute | solution.py:62
  26.5 9.0 %collective-permute-start.6 = (bf16[128,1024]{1,0:T(8,128)(2,1)S(1)}, bf16[128,1024]{1,0:T(8,128)(2,1)S(1)}, u32[]{:S(2)}, u32[]{:S(2)}) collective-permute-start(bf16[128,1024]{1,0:T(8,128)(2,1)S(1)} %get-tuple-element.40), channel_id=1, source_target_pairs={{0,4},{1,13},{2,6},{3,15},{4,8},{5,1},{6,10},{7,3},{8,12},{9,5},{1... | collective-permute-start | bytes 786440 | tf_op jit(solution)/shard_map/ppermute | solution.py:62
  33.7 5.0 %copy-start.1 = (bf16[256,1024]{1,0:T(8,128)(2,1)}, bf16[256,1024]{1,0:T(8,128)(2,1)S(1)}, u32[]{:S(2)}) copy-start(bf16[256,1024]{1,0:T(8,128)(2,1)S(1)} %collective-permute-done.2.refs_0_) | copy-start | bytes 1572868
  33.7 5.0 %copy-start.2 = (bf16[256,1024]{1,0:T(8,128)(2,1)}, bf16[256,1024]{1,0:T(8,128)(2,1)S(1)}, u32[]{:S(2)}) copy-start(bf16[256,1024]{1,0:T(8,128)(2,1)S(1)} %collective-permute-done.3.refs_1_) | copy-start | bytes 1572868
  35.6 5.5 %collective-permute-start.10 = (bf16[512,1024]{1,0:T(8,128)(2,1)S(1)}, bf16[512,1024]{1,0:T(8,128)(2,1)S(1)}, u32[]{:S(2)}, u32[]{:S(2)}) collective-permute-start(bf16[512,1024]{1,0:T(8,128)(2,1)S(1)} %constant_dynamic-update-slice_fusion.2.rows), channel_id=1, source_target_pairs={{0,1},{1,0},{2,3},{3,2},{4,5},{5,4},{6,7},{7,6},{8,9},{9,8},{10,11... | collective-permute-start | bytes 3145736 | tf_op jit(solution)/shard_map/ppermute | solution.py:62
  36.6 11.2 %collective-permute-start.12 = (bf16[256,1024]{1,0:T(8,128)(2,1)}, bf16[256,1024]{1,0:T(8,128)(2,1)}, u32[]{:S(2)}, u32[]{:S(2)}) collective-permute-start(bf16[256,1024]{1,0:T(8,128)(2,1)} %broadcast_select_fusion), channel_id=1, source_target_pairs={{0,32},{1,97},{2,34},{3,99},{4,36},{5,101},{6,38},{7,103},{8,40},{... | collective-permute-start | bytes 1572872 | tf_op jit(solution)/shard_map/ppermute | solution.py:62
  38.6 15.8 %collective-permute-start.13 = (bf16[384,1024]{1,0:T(8,128)(2,1)S(1)}, bf16[384,1024]{1,0:T(8,128)(2,1)}, u32[]{:S(2)}, u32[]{:S(2)}) collective-permute-start(bf16[384,1024]{1,0:T(8,128)(2,1)S(1)} %pad_maximum_fusion.rows3), channel_id=1, source_target_pairs={{0,1},{1,0},{2,3},{3,2},{4,5},{5,4},{6,7},{7,6},{8,9},{9,8},{10,11... | collective-permute-start | bytes 2359304 | tf_op jit(solution)/shard_map/ppermute | solution.py:62
  38.7 9.1 %collective-permute-start.11 = (bf16[128,1024]{1,0:T(8,128)(2,1)S(1)}, bf16[128,1024]{1,0:T(8,128)(2,1)S(1)}, u32[]{:S(2)}, u32[]{:S(2)}) collective-permute-start(bf16[128,1024]{1,0:T(8,128)(2,1)S(1)} %broadcast_select_fusion.1), channel_id=1, source_target_pairs={{0,4},{1,13},{2,6},{3,15},{4,8},{5,1},{6,10},{7,3},{8,12},{9,5},{1... | collective-permute-start | bytes 786440 | tf_op jit(solution)/shard_map/ppermute | solution.py:62
  47.8 6.7 %collective-permute-start.14 = (bf16[128,1024]{1,0:T(8,128)(2,1)S(1)}, bf16[128,1024]{1,0:T(8,128)(2,1)S(1)}, u32[]{:S(2)}, u32[]{:S(2)}) collective-permute-start(bf16[128,1024]{1,0:T(8,128)(2,1)S(1)} %collective-permute-done.11.facing), channel_id=1, source_target_pairs={{0,1},{1,0},{2,3},{3,2},{4,5},{5,4},{6,7},{7,6},{8,9},{9,8},{10,11... | collective-permute-start | bytes 786440 | tf_op jit(solution)/shard_map/ppermute | solution.py:62

commit v5 on v4

--- a/solution.py
+++ b/solution.py
@@ -33,13 +33,11 @@
 
 
 SWAP_CORE = moves(lambda x, y, z, c: (x, y, z, 1 - c))
+Y_FIRST = moves(lambda x, y, z, c: (x, (y + 1 + 2 * c) % 4, z, c))
+Y_SECOND = moves(lambda x, y, z, c: (x, (y + 3 + 2 * c) % 4, z, c))
+Z_FIRST = moves(lambda x, y, z, c: (x, y, (z + 1 + 2 * c) % 4, c))
+Z_SECOND = moves(lambda x, y, z, c: (x, y, (z + 3 + 2 * c) % 4, c))
 ACROSS_X = moves(lambda x, y, z, c: ((x + 2) % 4, y, z, c))
-Y_UP = moves(lambda x, y, z, c: (x, (y + 1) % 4, z, c))
-Y_DOWN = moves(lambda x, y, z, c: (x, (y + 3) % 4, z, c))
-Z_UP = moves(lambda x, y, z, c: (x, y, (z + 1) % 4, c))
-Z_DOWN = moves(lambda x, y, z, c: (x, y, (z + 3) % 4, c))
-Y_SPLIT = moves(lambda x, y, z, c: (x, (y + 1 + 2 * c) % 4, z, c))
-Z_SPLIT = moves(lambda x, y, z, c: (x, y, (z + 1 + 2 * c) % 4, c))
 
 
 def to_columns(flip):
@@ -105,7 +103,8 @@
 
 
 def z_of(step, where):
-    return lax.rem(where[0] + jnp.where(step == 1, 3, jnp.where(step == 2, 1, jnp.where(step == 3, 2, 0))), 4)
+    first = 3 - 2 * where[2]
+    return lax.rem(where[0] + jnp.where(step == 1, first, jnp.where(step == 2, 4 - first, 2 * (step // 3))), 4)
 
 
 def half_call(where, rows, swapped, pieces, before, name):
@@ -155,15 +154,17 @@
         return 0, z_of(step, where), 1 - where[1], 0, 0, 0
 
     vmem, anywhere = pl.BlockSpec(memory_space=pltpu.VMEM), pl.BlockSpec(memory_space=pl.ANY)
-    first_spec = pl.BlockSpec((WIDE, SPEC), lambda step, where: (0, 0))
     of_three = pl.BlockSpec((SHARD, SPEC), lambda step, where: (jnp.minimum(step, 2), 0))
+    of_three_swapped = pl.BlockSpec(
+        (SHARD, SPEC), lambda step, where: (jnp.where(step == 1, 2, jnp.where(step == 2, 1, 2 * (step // 3))), 0)
+    )
     whole = pl.BlockSpec((SHARD, SPEC), lambda step, where: (0, 0))
     return pl.pallas_call(
         last_kernel,
         grid_spec=pltpu.PrefetchScalarGridSpec(
             num_scalar_prefetch=1,
             grid=(4,),
-            in_specs=[of_three, whole, of_three, whole, first_spec, vmem, vmem, vmem, anywhere],
+            in_specs=[of_three, whole, of_three_swapped, whole, vmem, vmem, vmem, vmem, anywhere],
             out_specs=pl.BlockSpec((2, 1, 1, 2, SHARD, COLS), place_out),
         ),
         out_shape=jax.ShapeDtypeStruct(OUT, F32),
@@ -171,7 +172,7 @@
         compiler_params=pltpu.CompilerParams(vmem_limit_bytes=16 * 2**20),
         cost_estimate=pl.CostEstimate(flops=2**32, bytes_accessed=12 * 2**20, transcendentals=2048),
         name="across_rows",
-    )(where, *rows, in_hbm(first[0]), first[1], *second, before)
+    )(where, *rows, *first, *second, before)
 
 
 def in_hbm(value):
@@ -190,9 +191,9 @@
     return jnp.concatenate(shards, axis=0)
 
 
-def by_z(z, own, below, above, facing):
+def by_z(z, *placed):
     rows = jnp.zeros((4 * SHARD, SPEC), BF16)
-    for shard, up in ((own, 0), (below, 3), (above, 1), (facing, 2)):
+    for shard, up in placed:
         rows = lax.dynamic_update_slice(rows, shard, ((z + up) % 4 * SHARD, 0))
     return rows
 
@@ -205,22 +206,23 @@
         return stack(z, high, core, half, *[piece_spot((y + up) % 4, z, core, hx) % 4 for up, hx in steps])
 
     near_half = (y - z + 3) % 2
-    where = places(near_half, (3, low), (3, 1 - low), (1, low), (1, 1 - low))
+    one, two = 3 - 2 * core, 1 + 2 * core
+    where = places(near_half, (one, low), (one, 1 - low), (two, low), (two, 1 - low))
     where_far = places(1 - near_half, (0, low), (0, 1 - low), (2, low), (2, 1 - low))
-    a0, across, below, above, b0 = send(x, COLS_A), send(x, ACROSS_X), send(x, Z_UP), send(x, Z_DOWN), send(x, COLS_B)
+    a0, across, b0 = send(x, COLS_A), send(x, ACROSS_X), send(x, COLS_B)
+    z_first, z_second = send(x, Z_FIRST), send(x, Z_SECOND)
     a0, b0 = together(a0, b0)
     own = family(a0, b0)
-    up, down = send(own, Y_UP), send(own, Y_DOWN)
-    facing = send(jnp.where(core == 0, below, above), Z_SPLIT)
-    below_across, above_across = send(across, Z_UP), send(across, Z_DOWN)
-    onward = jnp.where(core == 0, below_across, above_across)
-    rows_across = family(across, below_across, above_across)
-    up, down, facing, rows_across, onward, far = together(up, down, facing, rows_across, onward, jnp.where(core == 0, up, down))
-    far = send(far, Y_SPLIT)
-    rows = by_z(z, x, below, above, facing)
+    y_first, y_second = send(own, Y_FIRST), send(own, Y_SECOND)
+    facing = send(z_first, Z_FIRST)
+    across_first, across_second = send(across, Z_FIRST), send(across, Z_SECOND)
+    rows_across = family(across, across_first, across_second)
+    y_first, y_second, facing, rows_across, across_first = together(y_first, y_second, facing, rows_across, across_first)
+    far = send(y_first, Y_FIRST)
+    rows = by_z(z, (x, 0), (z_first, one), (z_second, two), (facing, 2))
     swapped = send(rows, SWAP_CORE)
-    facing_across = send(onward, Z_SPLIT)
-    out, *first = half_call(where, rows, swapped, (up, down), None, "own_rows_near")
+    facing_across = send(across_first, Z_FIRST)
+    out, *first = half_call(where, rows, swapped, (y_first, y_second), None, "own_rows_near")
     out, facing_across, far = together(out, facing_across, far)
     swapped_across = send(rows_across, SWAP_CORE)
     facing_swapped = send(facing_across, SWAP_CORE)

time: 63.3 us -> 63.1 us (level)
  starting transfers between devices: 30.7 us -> 32.4 us
  local copies, waits for them, and re-layouts: 1.35 us -> 0.43 us
    ppermute x15, starting transfers between devices: 30.7 us -> 32.4 us  [send(): return lax.ppermute(value, AXES, pairs)]
    select_n x2 -> x0, other arithmetic: 0.97 us -> none  [the longest x1 0.94 us: shards(): jnp.where(core == 0, up, down)]
    concatenate x1, other arithmetic: 0.05 us -> 1 us  [family(): return jnp.concatenate(shards, axis=0)]
    dynamic_update_slice x3 -> x4, local copies, waits for them, and re-layouts: 1.02 us -> 0.1 us  [by_z(): rows = lax.dynamic_update_slice(rows, shard, ((z + up) % 4 * SHARD, 0))]
  transfers between devices with their start and end apart: 15 -> 15, of which waited for: 3 -> 3; matrix products, arithmetic and copies ran while one was open for 4% -> 2% of each run, Pallas kernels for 20% -> 21%
where the time goes in v5:
time: 63.1 us; the launch traced here: 62.9 us
  starting transfers between devices  32.4 us (51%)
  Pallas kernels  21.2 us (34%)
  waiting for transfers between devices  7.57 us (12%)
  other arithmetic  1 us (2%)
    ppermute x15, starting transfers between devices, send(): return lax.ppermute(value, AXES, pairs)  32.4 us
    pallas_call x2, Pallas kernels, half_call(): pl.pallas_call(half_kernel, grid_spec=pltpu.PrefetchScalarGridSpec(num_sc...  12.9 us
    pallas_call x1, Pallas kernels, last_call(): pl.pallas_call(last_kernel, grid_spec=pltpu.PrefetchScalarGridSpec(num_sc...  8.31 us
    ppermute x15, waiting for transfers between devices, send(): return lax.ppermute(value, AXES, pairs)  7.57 us
  transfers between devices with their start and end apart: 15, of which 3 were waited for; matrix products, arithmetic and copies ran while one was open for 2% of the time, Pallas kernels for 21%

profile of v5, /device:TPU:1, one launch (start us, length us, event | category | flops | bytes accessed | tf_op | source)
XLA Modules:
  0.0 62.9 jit_solution(6811514317429590636)
XLA Ops:
  0.0 0.0 copy-start.2
  0.0 6.3 %collective-permute-start = (bf16[128,1024]{1,0:T(8,128)(2,1)}, bf16[128,1024]{1,0:T(8,128)(2,1)S(1)}, u32[]{:S(2)}, u32[]{:S(2)}) collective-permute-start(bf16[128,1024]{1,0:T(8,128)(2,1)} %param.1), channel_id=1, source_target_pairs={{0,0},{1,64},{2,16},{3,80},{4,32},{5,96},{6,48},{7,112},{8,65},{9,... | collective-permute-start | bytes 786440 | tf_op jit(solution)/shard_map/ppermute | solution.py:60
  6.3 5.8 %collective-permute-start.1 = (bf16[128,1024]{1,0:T(8,128)(2,1)}, bf16[128,1024]{1,0:T(8,128)(2,1)S(1)}, u32[]{:S(2)}, u32[]{:S(2)}) collective-permute-start(bf16[128,1024]{1,0:T(8,128)(2,1)} %param.1), channel_id=1, source_target_pairs={{0,16},{1,80},{2,0},{3,64},{4,48},{5,112},{6,32},{7,96},{8,81},{9,... | collective-permute-start | bytes 786440 | tf_op jit(solution)/shard_map/ppermute | solution.py:60
  12.2 0.3 collective-permute-start.4
  12.4 1.2 %collective-permute-start.9 = (bf16[128,1024]{1,0:T(8,128)(2,1)}, bf16[128,1024]{1,0:T(8,128)(2,1)S(1)}, u32[]{:S(2)}, u32[]{:S(2)}) collective-permute-start(bf16[128,1024]{1,0:T(8,128)(2,1)} %param.1), channel_id=1, source_target_pairs={{0,12},{1,5},{2,14},{3,7},{4,0},{5,9},{6,2},{7,11},{8,4},{9,13},{1... | collective-permute-start | bytes 786440 | tf_op jit(solution)/shard_map/ppermute | solution.py:60
  13.6 0.8 %collective-permute-start.6 = (bf16[128,1024]{1,0:T(8,128)(2,1)}, bf16[128,1024]{1,0:T(8,128)(2,1)S(1)}, u32[]{:S(2)}, u32[]{:S(2)}) collective-permute-start(bf16[128,1024]{1,0:T(8,128)(2,1)} %param.1), channel_id=1, source_target_pairs={{0,2},{1,3},{2,0},{3,1},{4,6},{5,7},{6,4},{7,5},{8,10},{9,11},{10,... | collective-permute-start | bytes 786440 | tf_op jit(solution)/shard_map/ppermute | solution.py:60
  14.5 0.0 collective-permute-done
  14.5 1.3 %collective-permute-done.1 = bf16[128,1024]{1,0:T(8,128)(2,1)S(1)} collective-permute-done((bf16[128,1024]{1,0:T(8,128)(2,1)}, bf16[128,1024]{1,0:T(8,128)(2,1)S(1)}, u32[]{:S(2)}, u32[]{:S(2)}) %collective-permute-start.1) | collective-permute-done | bytes 262176 | tf_op jit(solution)/shard_map/ppermute | solution.py:60
  15.8 0.0 copy-start.1
  15.8 7.7 %collective-permute-start.2 = (bf16[256,1024]{1,0:T(8,128)(2,1)S(1)}, bf16[256,1024]{1,0:T(8,128)(2,1)}, u32[]{:S(2)}, u32[]{:S(2)}) collective-permute-start(bf16[256,1024]{1,0:T(8,128)(2,1)S(1)} %constant_dynamic-update-slice_fusion.refs_0_), channel_id=1, source_target_pairs={{0,32},{1,97},{2,34},{3,99},{4,36},{5,101},{6,38},{7,103},{8,40},{... | collective-permute-start | bytes 1572872 | tf_op jit(solution)/shard_map/ppermute | solution.py:60
  23.5 0.0 collective-permute-start.3
  23.5 0.0 collective-permute-done.6
  23.5 1.0 %collective-permute-start.7 = (bf16[128,1024]{1,0:T(8,128)(2,1)S(1)}, bf16[128,1024]{1,0:T(8,128)(2,1)S(1)}, u32[]{:S(2)}, u32[]{:S(2)}) collective-permute-start(bf16[128,1024]{1,0:T(8,128)(2,1)S(1)} %collective-permute-done.6), channel_id=1, source_target_pairs={{0,4},{1,13},{2,6},{3,15},{4,8},{5,1},{6,10},{7,3},{8,12},{9,5},{1... | collective-permute-start | bytes 786440 | tf_op jit(solution)/shard_map/ppermute | solution.py:60
  24.5 0.0 collective-permute-done.4
  24.5 0.5 collective-permute-start.8
  25.0 0.1 broadcast_in_dim.3
  25.1 0.0 copy-done.2
  25.3 0.0 collective-permute-done.9
  25.3 2.2 %collective-permute-start.5 = (bf16[128,1024]{1,0:T(8,128)(2,1)S(1)}, bf16[128,1024]{1,0:T(8,128)(2,1)S(1)}, u32[]{:S(2)}, u32[]{:S(2)}) collective-permute-start(bf16[128,1024]{1,0:T(8,128)(2,1)S(1)} %collective-permute-done.4), channel_id=1, source_target_pairs={{0,4},{1,13},{2,6},{3,15},{4,8},{5,1},{6,10},{7,3},{8,12},{9,5},{1... | collective-permute-start | bytes 786440 | tf_op jit(solution)/shard_map/ppermute | solution.py:60
  27.6 1.9 %collective-permute-done.7 = bf16[128,1024]{1,0:T(8,128)(2,1)S(1)} collective-permute-done((bf16[128,1024]{1,0:T(8,128)(2,1)S(1)}, bf16[128,1024]{1,0:T(8,128)(2,1)S(1)}, u32[]{:S(2)}, u32[]{:S(2)}) %collective-permute-start.7) | collective-permute-done | bytes 262176 | tf_op jit(solution)/shard_map/ppermute | solution.py:60
  29.5 4.3 %collective-permute-done.8 = bf16[128,1024]{1,0:T(8,128)(2,1)} collective-permute-done((bf16[128,1024]{1,0:T(8,128)(2,1)S(1)}, bf16[128,1024]{1,0:T(8,128)(2,1)}, u32[]{:S(2)}, u32[]{:S(2)}) %collective-permute-start.8) | collective-permute-done | bytes 262176 | tf_op jit(solution)/shard_map/ppermute | solution.py:60
  33.8 1.0 %pad_maximum_fusion.rows3 = bf16[384,1024]{1,0:T(8,128)(2,1)S(1)} fusion(bf16[128,1024]{1,0:T(8,128)(2,1)} %collective-permute-done.8, bf16[128,1024]{1,0:T(8,128)(2,1)S(1)} %collective-permute-done.7, bf16[128,1024]{1,0:T(8,128)(2,1)S(1)} %collective-permute-done.6), kind=kLoop, calls=%fused_computation | loop fusion | flops 2359296 | bytes 1572864 | tf_op jit(solution)/shard_map/concatenate | solution.py:191
  34.8 0.0 copy-done.1
  34.8 0.0 collective-permute-done.5
  34.8 0.0 collective-permute-done.2.refs_0_
  34.8 0.0 collective-permute-done.3.refs_1_
  34.8 2.5 %collective-permute-start.10 = (bf16[512,1024]{1,0:T(8,128)(2,1)S(1)}, bf16[512,1024]{1,0:T(8,128)(2,1)S(1)}, u32[]{:S(2)}, u32[]{:S(2)}) collective-permute-start(bf16[512,1024]{1,0:T(8,128)(2,1)S(1)} %constant_dynamic-update-slice_fusion.2.rows), channel_id=1, source_target_pairs={{0,1},{1,0},{2,3},{3,2},{4,5},{5,4},{6,7},{7,6},{8,9},{9,8},{10,11... | collective-permute-start | bytes 3145736 | tf_op jit(solution)/shard_map/ppermute | solution.py:60
  37.4 1.8 %collective-permute-start.12 = (bf16[256,1024]{1,0:T(8,128)(2,1)}, bf16[256,1024]{1,0:T(8,128)(2,1)}, u32[]{:S(2)}, u32[]{:S(2)}) collective-permute-start(bf16[256,1024]{1,0:T(8,128)(2,1)} %collective-permute-done.2.refs_0_), channel_id=1, source_target_pairs={{0,32},{1,97},{2,34},{3,99},{4,36},{5,101},{6,38},{7,103},{8,40},{... | collective-permute-start | bytes 1572872 | tf_op jit(solution)/shard_map/ppermute | solution.py:60
  39.2 0.0 collective-permute-start.13
  39.2 1.3 %collective-permute-start.11 = (bf16[128,1024]{1,0:T(8,128)(2,1)S(1)}, bf16[128,1024]{1,0:T(8,128)(2,1)S(1)}, u32[]{:S(2)}, u32[]{:S(2)}) collective-permute-start(bf16[128,1024]{1,0:T(8,128)(2,1)S(1)} %collective-permute-done.7), channel_id=1, source_target_pairs={{0,4},{1,13},{2,6},{3,15},{4,8},{5,1},{6,10},{7,3},{8,12},{9,5},{1... | collective-permute-start | bytes 786440 | tf_op jit(solution)/shard_map/ppermute | solution.py:60
  40.5 0.1 stack.56.where
  40.6 0.0 collective-permute-done.10.swapped
  40.6 6.6 %own_rows_near.1 = (f32[2,4,2,2,128,1024]{5,4,3,2,1,0:T(8,128)}, bf16[512,1024]{1,0:T(8,128)(2,1)}, f32[8,512]{1,0:T(8,128)S(1)}) custom-call(s32[8]{0:T(128)S(1)} %stack.56.where, bf16[512,1024]{1,0:T(8,128)(2,1)S(1)} %constant_dynamic-update-slice_fusion.2.rows, bf16[512,1024]{1,0:T(8,128)(2,1)S(1)} %collective-permute-done.10.swapped, ...), custom_call_target="tpu_custom_call" | custom-call | flops 2147483648 | bytes 7340032 | tf_op jit(solution)/shard_map/own_rows_near/pallas_call | solution.py:122
  47.2 0.0 collective-permute-done.11.facing
  47.2 0.0 collective-permute-done.12.refs_1_
  47.2 0.9 %collective-permute-start.14 = (bf16[128,1024]{1,0:T(8,128)(2,1)S(1)}, bf16[128,1024]{1,0:T(8,128)(2,1)S(1)}, u32[]{:S(2)}, u32[]{:S(2)}) collective-permute-start(bf16[128,1024]{1,0:T(8,128)(2,1)S(1)} %collective-permute-done.11.facing), channel_id=1, source_target_pairs={{0,1},{1,0},{2,3},{3,2},{4,5},{5,4},{6,7},{7,6},{8,9},{9,8},{10,11... | collective-permute-start | bytes 786440 | tf_op jit(solution)/shard_map/ppermute | solution.py:60
  48.2 0.1 stack.62.where
  48.2 0.0 copy-start
  48.2 6.3 %own_rows_far.1 = (f32[2,4,2,2,128,1024]{5,4,3,2,1,0:T(8,128)}, bf16[512,1024]{1,0:T(8,128)(2,1)S(1)}, f32[8,512]{1,0:T(8,128)S(1)}) custom-call(s32[8]{0:T(128)S(1)} %stack.62.where, bf16[512,1024]{1,0:T(8,128)(2,1)S(1)} %constant_dynamic-update-slice_fusion.2.rows, ...), custom_call_target="tpu_custom_call", output_to_operand_aliasing={{0}: (5, {})} | custom-call | flops 2147483648 | bytes 7340032 | tf_op jit(solution)/shard_map/own_rows_far/pallas_call | solution.py:122
  54.5 0.0 collective-permute-done.13.swapped3
  54.5 0.0 collective-permute-done.14.swapped_facing
  54.5 0.0 copy-done
  54.5 8.3 %across_rows.1 = f32[2,4,2,2,128,1024]{5,4,3,2,1,0:T(8,128)} custom-call(s32[8]{0:T(128)S(1)} %stack.56.where, bf16[384,1024]{1,0:T(8,128)(2,1)S(1)} %pad_maximum_fusion.rows3, bf16[128,1024]{1,0:T(8,128)(2,1)S(1)} %collective-permute-done.11.facing, bf16[384,1024]{1,0:T(8,128)(2,1)} %collective-permute-done.13.swapped3, ...), custom_call_target="tpu_custom_call", output_to_operand_aliasing={{}: (9, {})} | custom-call | flops 4294967296 | bytes 12582912 | tf_op jit(solution)/shard_map/across_rows/pallas_call | solution.py:162
  (6 shorter events, 0.1 us)
Async XLA Ops:
  0.0 25.1 %copy-start.2 = (bf16[128,1024]{1,0:T(8,128)(2,1)S(1)}, bf16[128,1024]{1,0:T(8,128)(2,1)}, u32[]{:S(2)}) copy-start(bf16[128,1024]{1,0:T(8,128)(2,1)} %param.1) | copy-start | bytes 786436
  0.0 14.5 %collective-permute-start = (bf16[128,1024]{1,0:T(8,128)(2,1)}, bf16[128,1024]{1,0:T(8,128)(2,1)S(1)}, u32[]{:S(2)}, u32[]{:S(2)}) collective-permute-start(bf16[128,1024]{1,0:T(8,128)(2,1)} %param.1), channel_id=1, source_target_pairs={{0,0},{1,64},{2,16},{3,80},{4,32},{5,96},{6,48},{7,112},{8,65},{9,... | collective-permute-start | bytes 786440 | tf_op jit(solution)/shard_map/ppermute | solution.py:60
  6.3 9.4 %collective-permute-start.1 = (bf16[128,1024]{1,0:T(8,128)(2,1)}, bf16[128,1024]{1,0:T(8,128)(2,1)S(1)}, u32[]{:S(2)}, u32[]{:S(2)}) collective-permute-start(bf16[128,1024]{1,0:T(8,128)(2,1)} %param.1), channel_id=1, source_target_pairs={{0,16},{1,80},{2,0},{3,64},{4,48},{5,112},{6,32},{7,96},{8,81},{9,... | collective-permute-start | bytes 786440 | tf_op jit(solution)/shard_map/ppermute | solution.py:60
  12.2 12.3 %collective-permute-start.4 = (bf16[128,1024]{1,0:T(8,128)(2,1)}, bf16[128,1024]{1,0:T(8,128)(2,1)S(1)}, u32[]{:S(2)}, u32[]{:S(2)}) collective-permute-start(bf16[128,1024]{1,0:T(8,128)(2,1)} %param.1), channel_id=1, source_target_pairs={{0,4},{1,13},{2,6},{3,15},{4,8},{5,1},{6,10},{7,3},{8,12},{9,5},{1... | collective-permute-start | bytes 786440 | tf_op jit(solution)/shard_map/ppermute | solution.py:60
  12.4 12.8 %collective-permute-start.9 = (bf16[128,1024]{1,0:T(8,128)(2,1)}, bf16[128,1024]{1,0:T(8,128)(2,1)S(1)}, u32[]{:S(2)}, u32[]{:S(2)}) collective-permute-start(bf16[128,1024]{1,0:T(8,128)(2,1)} %param.1), channel_id=1, source_target_pairs={{0,12},{1,5},{2,14},{3,7},{4,0},{5,9},{6,2},{7,11},{8,4},{9,13},{1... | collective-permute-start | bytes 786440 | tf_op jit(solution)/shard_map/ppermute | solution.py:60
  13.6 9.9 %collective-permute-start.6 = (bf16[128,1024]{1,0:T(8,128)(2,1)}, bf16[128,1024]{1,0:T(8,128)(2,1)S(1)}, u32[]{:S(2)}, u32[]{:S(2)}) collective-permute-start(bf16[128,1024]{1,0:T(8,128)(2,1)} %param.1), channel_id=1, source_target_pairs={{0,2},{1,3},{2,0},{3,1},{4,6},{5,7},{6,4},{7,5},{8,10},{9,11},{10,... | collective-permute-start | bytes 786440 | tf_op jit(solution)/shard_map/ppermute | solution.py:60
  15.8 18.9 %copy-start.1 = (bf16[256,1024]{1,0:T(8,128)(2,1)}, bf16[256,1024]{1,0:T(8,128)(2,1)S(1)}, u32[]{:S(2)}) copy-start(bf16[256,1024]{1,0:T(8,128)(2,1)S(1)} %constant_dynamic-update-slice_fusion.refs_0_) | copy-start | bytes 1572868
  15.8 19.0 %collective-permute-start.2 = (bf16[256,1024]{1,0:T(8,128)(2,1)S(1)}, bf16[256,1024]{1,0:T(8,128)(2,1)}, u32[]{:S(2)}, u32[]{:S(2)}) collective-permute-start(bf16[256,1024]{1,0:T(8,128)(2,1)S(1)} %constant_dynamic-update-slice_fusion.refs_0_), channel_id=1, source_target_pairs={{0,32},{1,97},{2,34},{3,99},{4,36},{5,101},{6,38},{7,103},{8,40},{... | collective-permute-start | bytes 1572872 | tf_op jit(solution)/shard_map/ppermute | solution.py:60
  23.5 11.3 %collective-permute-start.3 = (bf16[256,1024]{1,0:T(8,128)(2,1)S(1)}, bf16[256,1024]{1,0:T(8,128)(2,1)}, u32[]{:S(2)}, u32[]{:S(2)}) collective-permute-start(bf16[256,1024]{1,0:T(8,128)(2,1)S(1)} %constant_dynamic-update-slice_fusion.refs_0_), channel_id=1, source_target_pairs={{0,96},{1,33},{2,98},{3,35},{4,100},{5,37},{6,102},{7,39},{8,104},... | collective-permute-start | bytes 1572872 | tf_op jit(solution)/shard_map/ppermute | solution.py:60
  23.5 5.9 %collective-permute-start.7 = (bf16[128,1024]{1,0:T(8,128)(2,1)S(1)}, bf16[128,1024]{1,0:T(8,128)(2,1)S(1)}, u32[]{:S(2)}, u32[]{:S(2)}) collective-permute-start(bf16[128,1024]{1,0:T(8,128)(2,1)S(1)} %collective-permute-done.6), channel_id=1, source_target_pairs={{0,4},{1,13},{2,6},{3,15},{4,8},{5,1},{6,10},{7,3},{8,12},{9,5},{1... | collective-permute-start | bytes 786440 | tf_op jit(solution)/shard_map/ppermute | solution.py:60
  24.5 9.3 %collective-permute-start.8 = (bf16[128,1024]{1,0:T(8,128)(2,1)S(1)}, bf16[128,1024]{1,0:T(8,128)(2,1)}, u32[]{:S(2)}, u32[]{:S(2)}) collective-permute-start(bf16[128,1024]{1,0:T(8,128)(2,1)S(1)} %collective-permute-done.6), channel_id=1, source_target_pairs={{0,12},{1,5},{2,14},{3,7},{4,0},{5,9},{6,2},{7,11},{8,4},{9,13},{1... | collective-permute-start | bytes 786440 | tf_op jit(solution)/shard_map/ppermute | solution.py:60
  25.3 9.5 %collective-permute-start.5 = (bf16[128,1024]{1,0:T(8,128)(2,1)S(1)}, bf16[128,1024]{1,0:T(8,128)(2,1)S(1)}, u32[]{:S(2)}, u32[]{:S(2)}) collective-permute-start(bf16[128,1024]{1,0:T(8,128)(2,1)S(1)} %collective-permute-done.4), channel_id=1, source_target_pairs={{0,4},{1,13},{2,6},{3,15},{4,8},{5,1},{6,10},{7,3},{8,12},{9,5},{1... | collective-permute-start | bytes 786440 | tf_op jit(solution)/shard_map/ppermute | solution.py:60
  34.8 5.7 %collective-permute-start.10 = (bf16[512,1024]{1,0:T(8,128)(2,1)S(1)}, bf16[512,1024]{1,0:T(8,128)(2,1)S(1)}, u32[]{:S(2)}, u32[]{:S(2)}) collective-permute-start(bf16[512,1024]{1,0:T(8,128)(2,1)S(1)} %constant_dynamic-update-slice_fusion.2.rows), channel_id=1, source_target_pairs={{0,1},{1,0},{2,3},{3,2},{4,5},{5,4},{6,7},{7,6},{8,9},{9,8},{10,11... | collective-permute-start | bytes 3145736 | tf_op jit(solution)/shard_map/ppermute | solution.py:60
  37.4 9.9 %collective-permute-start.12 = (bf16[256,1024]{1,0:T(8,128)(2,1)}, bf16[256,1024]{1,0:T(8,128)(2,1)}, u32[]{:S(2)}, u32[]{:S(2)}) collective-permute-start(bf16[256,1024]{1,0:T(8,128)(2,1)} %collective-permute-done.2.refs_0_), channel_id=1, source_target_pairs={{0,32},{1,97},{2,34},{3,99},{4,36},{5,101},{6,38},{7,103},{8,40},{... | collective-permute-start | bytes 1572872 | tf_op jit(solution)/shard_map/ppermute | solution.py:60
  39.2 15.4 %collective-permute-start.13 = (bf16[384,1024]{1,0:T(8,128)(2,1)S(1)}, bf16[384,1024]{1,0:T(8,128)(2,1)}, u32[]{:S(2)}, u32[]{:S(2)}) collective-permute-start(bf16[384,1024]{1,0:T(8,128)(2,1)S(1)} %pad_maximum_fusion.rows3), channel_id=1, source_target_pairs={{0,1},{1,0},{2,3},{3,2},{4,5},{5,4},{6,7},{7,6},{8,9},{9,8},{10,11... | collective-permute-start | bytes 2359304 | tf_op jit(solution)/shard_map/ppermute | solution.py:60
  39.2 8.1 %collective-permute-start.11 = (bf16[128,1024]{1,0:T(8,128)(2,1)S(1)}, bf16[128,1024]{1,0:T(8,128)(2,1)S(1)}, u32[]{:S(2)}, u32[]{:S(2)}) collective-permute-start(bf16[128,1024]{1,0:T(8,128)(2,1)S(1)} %collective-permute-done.7), channel_id=1, source_target_pairs={{0,4},{1,13},{2,6},{3,15},{4,8},{5,1},{6,10},{7,3},{8,12},{9,5},{1... | collective-permute-start | bytes 786440 | tf_op jit(solution)/shard_map/ppermute | solution.py:60
  47.2 7.3 %collective-permute-start.14 = (bf16[128,1024]{1,0:T(8,128)(2,1)S(1)}, bf16[128,1024]{1,0:T(8,128)(2,1)S(1)}, u32[]{:S(2)}, u32[]{:S(2)}) collective-permute-start(bf16[128,1024]{1,0:T(8,128)(2,1)S(1)} %collective-permute-done.11.facing), channel_id=1, source_target_pairs={{0,1},{1,0},{2,3},{3,2},{4,5},{5,4},{6,7},{7,6},{8,9},{9,8},{10,11... | collective-permute-start | bytes 786440 | tf_op jit(solution)/shard_map/ppermute | solution.py:60
  48.2 6.3 %copy-start = (bf16[512,1024]{1,0:T(8,128)(2,1)S(1)}, bf16[512,1024]{1,0:T(8,128)(2,1)}, u32[]{:S(2)}) copy-start(bf16[512,1024]{1,0:T(8,128)(2,1)} %get-tuple-element.30.b0) | copy-start | bytes 3145732

commit v6 on v5

--- a/solution.py
+++ b/solution.py
@@ -36,6 +36,7 @@
 Y_FIRST = moves(lambda x, y, z, c: (x, (y + 1 + 2 * c) % 4, z, c))
 Y_SECOND = moves(lambda x, y, z, c: (x, (y + 3 + 2 * c) % 4, z, c))
 Z_FIRST = moves(lambda x, y, z, c: (x, y, (z + 1 + 2 * c) % 4, c))
+Z_FIRST_CROSS = moves(lambda x, y, z, c: (x, y, (z + 1 + 2 * c) % 4, 1 - c))
 Z_SECOND = moves(lambda x, y, z, c: (x, y, (z + 3 + 2 * c) % 4, c))
 ACROSS_X = moves(lambda x, y, z, c: ((x + 2) % 4, y, z, c))
 
@@ -221,11 +222,10 @@
     far = send(y_first, Y_FIRST)
     rows = by_z(z, (x, 0), (z_first, one), (z_second, two), (facing, 2))
     swapped = send(rows, SWAP_CORE)
-    facing_across = send(across_first, Z_FIRST)
+    facing_across, facing_swapped = send(across_first, Z_FIRST), send(across_first, Z_FIRST_CROSS)
     out, *first = half_call(where, rows, swapped, (y_first, y_second), None, "own_rows_near")
-    out, facing_across, far = together(out, facing_across, far)
+    out, facing_across, facing_swapped, far = together(out, facing_across, facing_swapped, far)
     swapped_across = send(rows_across, SWAP_CORE)
-    facing_swapped = send(facing_across, SWAP_CORE)
     out, *second = half_call(where_far, rows, swapped, (own, far), out, "own_rows_far")
     out = last_call(where, (rows_across, facing_across, swapped_across, facing_swapped), first, second, out)
     return out.reshape(2, 4 * 4 * SHARD, COLS)

time: 63.1 us -> 63.1 us (level)
  transfers between devices with their start and end apart: 15 -> 15, of which waited for: 3 -> 4; matrix products, arithmetic and copies ran while one was open for 2% -> 2% of each run, Pallas kernels for 21% -> 21%
where the time goes in v6:
time: 63.1 us; the launch traced here: 62.9 us
  starting transfers between devices  32.2 us (51%)
  Pallas kernels  21.2 us (34%)
  waiting for transfers between devices  7.8 us (12%)
  other arithmetic  1 us (2%)
    ppermute x15, starting transfers between devices, send(): return lax.ppermute(value, AXES, pairs)  32.2 us
    pallas_call x2, Pallas kernels, half_call(): pl.pallas_call(half_kernel, grid_spec=pltpu.PrefetchScalarGridSpec(num_sc...  12.9 us
    pallas_call x1, Pallas kernels, last_call(): pl.pallas_call(last_kernel, grid_spec=pltpu.PrefetchScalarGridSpec(num_sc...  8.26 us
    ppermute x15, waiting for transfers between devices, send(): return lax.ppermute(value, AXES, pairs)  7.8 us
  transfers between devices with their start and end apart: 15, of which 4 were waited for; matrix products, arithmetic and copies ran while one was open for 2% of the time, Pallas kernels for 21%

profile of v6, /device:TPU:1, one launch (start us, length us, event | category | flops | bytes accessed | tf_op | source)
XLA Modules:
  0.0 62.9 jit_solution(12943658970535222956)
XLA Ops:
  0.0 0.0 copy-start.2
  0.0 6.3 %collective-permute-start = (bf16[128,1024]{1,0:T(8,128)(2,1)}, bf16[128,1024]{1,0:T(8,128)(2,1)S(1)}, u32[]{:S(2)}, u32[]{:S(2)}) collective-permute-start(bf16[128,1024]{1,0:T(8,128)(2,1)} %param.1), channel_id=1, source_target_pairs={{0,0},{1,64},{2,16},{3,80},{4,32},{5,96},{6,48},{7,112},{8,65},{9,... | collective-permute-start | bytes 786440 | tf_op jit(solution)/shard_map/ppermute | solution.py:61
  6.3 5.8 %collective-permute-start.1 = (bf16[128,1024]{1,0:T(8,128)(2,1)}, bf16[128,1024]{1,0:T(8,128)(2,1)S(1)}, u32[]{:S(2)}, u32[]{:S(2)}) collective-permute-start(bf16[128,1024]{1,0:T(8,128)(2,1)} %param.1), channel_id=1, source_target_pairs={{0,16},{1,80},{2,0},{3,64},{4,48},{5,112},{6,32},{7,96},{8,81},{9,... | collective-permute-start | bytes 786440 | tf_op jit(solution)/shard_map/ppermute | solution.py:61
  12.2 0.3 collective-permute-start.4
  12.4 1.2 %collective-permute-start.9 = (bf16[128,1024]{1,0:T(8,128)(2,1)}, bf16[128,1024]{1,0:T(8,128)(2,1)S(1)}, u32[]{:S(2)}, u32[]{:S(2)}) collective-permute-start(bf16[128,1024]{1,0:T(8,128)(2,1)} %param.1), channel_id=1, source_target_pairs={{0,12},{1,5},{2,14},{3,7},{4,0},{5,9},{6,2},{7,11},{8,4},{9,13},{1... | collective-permute-start | bytes 786440 | tf_op jit(solution)/shard_map/ppermute | solution.py:61
  13.6 0.8 %collective-permute-start.6 = (bf16[128,1024]{1,0:T(8,128)(2,1)}, bf16[128,1024]{1,0:T(8,128)(2,1)S(1)}, u32[]{:S(2)}, u32[]{:S(2)}) collective-permute-start(bf16[128,1024]{1,0:T(8,128)(2,1)} %param.1), channel_id=1, source_target_pairs={{0,2},{1,3},{2,0},{3,1},{4,6},{5,7},{6,4},{7,5},{8,10},{9,11},{10,... | collective-permute-start | bytes 786440 | tf_op jit(solution)/shard_map/ppermute | solution.py:61
  14.5 0.0 collective-permute-done
  14.5 1.3 %collective-permute-done.1 = bf16[128,1024]{1,0:T(8,128)(2,1)S(1)} collective-permute-done((bf16[128,1024]{1,0:T(8,128)(2,1)}, bf16[128,1024]{1,0:T(8,128)(2,1)S(1)}, u32[]{:S(2)}, u32[]{:S(2)}) %collective-permute-start.1) | collective-permute-done | bytes 262176 | tf_op jit(solution)/shard_map/ppermute | solution.py:61
  15.8 0.0 copy-start.1
  15.8 7.7 %collective-permute-start.2 = (bf16[256,1024]{1,0:T(8,128)(2,1)S(1)}, bf16[256,1024]{1,0:T(8,128)(2,1)}, u32[]{:S(2)}, u32[]{:S(2)}) collective-permute-start(bf16[256,1024]{1,0:T(8,128)(2,1)S(1)} %constant_dynamic-update-slice_fusion.refs_0_), channel_id=1, source_target_pairs={{0,32},{1,97},{2,34},{3,99},{4,36},{5,101},{6,38},{7,103},{8,40},{... | collective-permute-start | bytes 1572872 | tf_op jit(solution)/shard_map/ppermute | solution.py:61
  23.5 0.0 collective-permute-start.3
  23.5 0.0 collective-permute-done.6
  23.5 1.0 %collective-permute-start.7 = (bf16[128,1024]{1,0:T(8,128)(2,1)S(1)}, bf16[128,1024]{1,0:T(8,128)(2,1)S(1)}, u32[]{:S(2)}, u32[]{:S(2)}) collective-permute-start(bf16[128,1024]{1,0:T(8,128)(2,1)S(1)} %collective-permute-done.6), channel_id=1, source_target_pairs={{0,4},{1,13},{2,6},{3,15},{4,8},{5,1},{6,10},{7,3},{8,12},{9,5},{1... | collective-permute-start | bytes 786440 | tf_op jit(solution)/shard_map/ppermute | solution.py:61
  24.5 0.0 collective-permute-done.4
  24.5 0.5 collective-permute-start.8
  25.0 0.1 broadcast_in_dim.3
  25.1 0.0 copy-done.2
  25.3 0.0 collective-permute-done.9
  25.3 2.2 %collective-permute-start.5 = (bf16[128,1024]{1,0:T(8,128)(2,1)S(1)}, bf16[128,1024]{1,0:T(8,128)(2,1)S(1)}, u32[]{:S(2)}, u32[]{:S(2)}) collective-permute-start(bf16[128,1024]{1,0:T(8,128)(2,1)S(1)} %collective-permute-done.4), channel_id=1, source_target_pairs={{0,4},{1,13},{2,6},{3,15},{4,8},{5,1},{6,10},{7,3},{8,12},{9,5},{1... | collective-permute-start | bytes 786440 | tf_op jit(solution)/shard_map/ppermute | solution.py:61
  27.6 1.9 %collective-permute-done.7 = bf16[128,1024]{1,0:T(8,128)(2,1)S(1)} collective-permute-done((bf16[128,1024]{1,0:T(8,128)(2,1)S(1)}, bf16[128,1024]{1,0:T(8,128)(2,1)S(1)}, u32[]{:S(2)}, u32[]{:S(2)}) %collective-permute-start.7) | collective-permute-done | bytes 262176 | tf_op jit(solution)/shard_map/ppermute | solution.py:61
  29.5 0.0 copy-start.3
  29.5 4.3 %collective-permute-done.8 = bf16[128,1024]{1,0:T(8,128)(2,1)} collective-permute-done((bf16[128,1024]{1,0:T(8,128)(2,1)S(1)}, bf16[128,1024]{1,0:T(8,128)(2,1)}, u32[]{:S(2)}, u32[]{:S(2)}) %collective-permute-start.8) | collective-permute-done | bytes 262176 | tf_op jit(solution)/shard_map/ppermute | solution.py:61
  33.8 1.0 %pad_maximum_fusion.rows3 = bf16[384,1024]{1,0:T(8,128)(2,1)S(1)} fusion(bf16[128,1024]{1,0:T(8,128)(2,1)} %collective-permute-done.8, bf16[128,1024]{1,0:T(8,128)(2,1)S(1)} %collective-permute-done.7, bf16[128,1024]{1,0:T(8,128)(2,1)S(1)} %collective-permute-done.6), kind=kLoop, calls=%fused_computation | loop fusion | flops 2359296 | bytes 1572864 | tf_op jit(solution)/shard_map/concatenate | solution.py:192
  34.8 0.0 copy-done.1
  34.8 0.0 collective-permute-done.5
  34.8 0.0 collective-permute-done.2.refs_0_
  34.8 0.0 collective-permute-done.3.refs_1_
  34.8 0.0 copy-done.3
  34.9 2.5 %collective-permute-start.10 = (bf16[512,1024]{1,0:T(8,128)(2,1)S(1)}, bf16[512,1024]{1,0:T(8,128)(2,1)S(1)}, u32[]{:S(2)}, u32[]{:S(2)}) collective-permute-start(bf16[512,1024]{1,0:T(8,128)(2,1)S(1)} %constant_dynamic-update-slice_fusion.2.rows), channel_id=1, source_target_pairs={{0,1},{1,0},{2,3},{3,2},{4,5},{5,4},{6,7},{7,6},{8,9},{9,8},{10,11... | collective-permute-start | bytes 3145736 | tf_op jit(solution)/shard_map/ppermute | solution.py:61
  37.4 0.1 collective-permute-start.14
  37.5 1.8 %collective-permute-start.13 = (bf16[256,1024]{1,0:T(8,128)(2,1)}, bf16[256,1024]{1,0:T(8,128)(2,1)}, u32[]{:S(2)}, u32[]{:S(2)}) collective-permute-start(bf16[256,1024]{1,0:T(8,128)(2,1)} %collective-permute-done.2.refs_0_), channel_id=1, source_target_pairs={{0,32},{1,97},{2,34},{3,99},{4,36},{5,101},{6,38},{7,103},{8,40},{... | collective-permute-start | bytes 1572872 | tf_op jit(solution)/shard_map/ppermute | solution.py:61
  39.3 1.3 %collective-permute-start.11 = (bf16[128,1024]{1,0:T(8,128)(2,1)}, bf16[128,1024]{1,0:T(8,128)(2,1)S(1)}, u32[]{:S(2)}, u32[]{:S(2)}) collective-permute-start(bf16[128,1024]{1,0:T(8,128)(2,1)} %copy-done.3), channel_id=1, source_target_pairs={{0,4},{1,13},{2,6},{3,15},{4,8},{5,1},{6,10},{7,3},{8,12},{9,5},{1... | collective-permute-start | bytes 786440 | tf_op jit(solution)/shard_map/ppermute | solution.py:61
  40.6 0.6 %collective-permute-start.12 = (bf16[128,1024]{1,0:T(8,128)(2,1)}, bf16[128,1024]{1,0:T(8,128)(2,1)S(1)}, u32[]{:S(2)}, u32[]{:S(2)}) collective-permute-start(bf16[128,1024]{1,0:T(8,128)(2,1)} %copy-done.3), channel_id=1, source_target_pairs={{0,5},{1,12},{2,7},{3,14},{4,9},{5,0},{6,11},{7,2},{8,13},{9,4},{1... | collective-permute-start | bytes 786440 | tf_op jit(solution)/shard_map/ppermute | solution.py:61
  41.2 0.1 stack.62.where
  41.3 0.1 stack.56.where
  41.4 0.0 collective-permute-done.10.swapped
  41.4 6.6 %own_rows_near.1 = (f32[2,4,2,2,128,1024]{5,4,3,2,1,0:T(8,128)}, bf16[512,1024]{1,0:T(8,128)(2,1)}, f32[8,512]{1,0:T(8,128)S(1)}) custom-call(s32[8]{0:T(128)S(1)} %stack.56.where, bf16[512,1024]{1,0:T(8,128)(2,1)S(1)} %constant_dynamic-update-slice_fusion.2.rows, bf16[512,1024]{1,0:T(8,128)(2,1)S(1)} %collective-permute-done.10.swapped, ...), custom_call_target="tpu_custom_call" | custom-call | flops 2147483648 | bytes 7340032 | tf_op jit(solution)/shard_map/own_rows_near/pallas_call | solution.py:123
  48.1 0.0 collective-permute-done.11.facing
  48.1 0.2 collective-permute-done.12.swapped_facing
  48.3 0.0 collective-permute-done.13.refs_1_
  48.3 0.0 copy-start
  48.3 6.3 %own_rows_far.1 = (f32[2,4,2,2,128,1024]{5,4,3,2,1,0:T(8,128)}, bf16[512,1024]{1,0:T(8,128)(2,1)S(1)}, f32[8,512]{1,0:T(8,128)S(1)}) custom-call(s32[8]{0:T(128)S(1)} %stack.62.where, bf16[512,1024]{1,0:T(8,128)(2,1)S(1)} %constant_dynamic-update-slice_fusion.2.rows, ...), custom_call_target="tpu_custom_call", output_to_operand_aliasing={{0}: (5, {})} | custom-call | flops 2147483648 | bytes 7340032 | tf_op jit(solution)/shard_map/own_rows_far/pallas_call | solution.py:123
  54.6 0.0 collective-permute-done.14.swapped3
  54.6 0.0 copy-done
  54.6 8.3 %across_rows.1 = f32[2,4,2,2,128,1024]{5,4,3,2,1,0:T(8,128)} custom-call(s32[8]{0:T(128)S(1)} %stack.56.where, bf16[384,1024]{1,0:T(8,128)(2,1)S(1)} %pad_maximum_fusion.rows3, bf16[128,1024]{1,0:T(8,128)(2,1)S(1)} %collective-permute-done.11.facing, bf16[384,1024]{1,0:T(8,128)(2,1)} %collective-permute-done.14.swapped3, ...), custom_call_target="tpu_custom_call", output_to_operand_aliasing={{}: (9, {})} | custom-call | flops 4294967296 | bytes 12582912 | tf_op jit(solution)/shard_map/across_rows/pallas_call | solution.py:163
  (6 shorter events, 0.1 us)
Async XLA Ops:
  0.0 25.1 %copy-start.2 = (bf16[128,1024]{1,0:T(8,128)(2,1)S(1)}, bf16[128,1024]{1,0:T(8,128)(2,1)}, u32[]{:S(2)}) copy-start(bf16[128,1024]{1,0:T(8,128)(2,1)} %param.1) | copy-start | bytes 786436
  0.0 14.5 %collective-permute-start = (bf16[128,1024]{1,0:T(8,128)(2,1)}, bf16[128,1024]{1,0:T(8,128)(2,1)S(1)}, u32[]{:S(2)}, u32[]{:S(2)}) collective-permute-start(bf16[128,1024]{1,0:T(8,128)(2,1)} %param.1), channel_id=1, source_target_pairs={{0,0},{1,64},{2,16},{3,80},{4,32},{5,96},{6,48},{7,112},{8,65},{9,... | collective-permute-start | bytes 786440 | tf_op jit(solution)/shard_map/ppermute | solution.py:61
  6.3 9.4 %collective-permute-start.1 = (bf16[128,1024]{1,0:T(8,128)(2,1)}, bf16[128,1024]{1,0:T(8,128)(2,1)S(1)}, u32[]{:S(2)}, u32[]{:S(2)}) collective-permute-start(bf16[128,1024]{1,0:T(8,128)(2,1)} %param.1), channel_id=1, source_target_pairs={{0,16},{1,80},{2,0},{3,64},{4,48},{5,112},{6,32},{7,96},{8,81},{9,... | collective-permute-start | bytes 786440 | tf_op jit(solution)/shard_map/ppermute | solution.py:61
  12.2 12.3 %collective-permute-start.4 = (bf16[128,1024]{1,0:T(8,128)(2,1)}, bf16[128,1024]{1,0:T(8,128)(2,1)S(1)}, u32[]{:S(2)}, u32[]{:S(2)}) collective-permute-start(bf16[128,1024]{1,0:T(8,128)(2,1)} %param.1), channel_id=1, source_target_pairs={{0,4},{1,13},{2,6},{3,15},{4,8},{5,1},{6,10},{7,3},{8,12},{9,5},{1... | collective-permute-start | bytes 786440 | tf_op jit(solution)/shard_map/ppermute | solution.py:61
  12.4 12.8 %collective-permute-start.9 = (bf16[128,1024]{1,0:T(8,128)(2,1)}, bf16[128,1024]{1,0:T(8,128)(2,1)S(1)}, u32[]{:S(2)}, u32[]{:S(2)}) collective-permute-start(bf16[128,1024]{1,0:T(8,128)(2,1)} %param.1), channel_id=1, source_target_pairs={{0,12},{1,5},{2,14},{3,7},{4,0},{5,9},{6,2},{7,11},{8,4},{9,13},{1... | collective-permute-start | bytes 786440 | tf_op jit(solution)/shard_map/ppermute | solution.py:61
  13.6 9.9 %collective-permute-start.6 = (bf16[128,1024]{1,0:T(8,128)(2,1)}, bf16[128,1024]{1,0:T(8,128)(2,1)S(1)}, u32[]{:S(2)}, u32[]{:S(2)}) collective-permute-start(bf16[128,1024]{1,0:T(8,128)(2,1)} %param.1), channel_id=1, source_target_pairs={{0,2},{1,3},{2,0},{3,1},{4,6},{5,7},{6,4},{7,5},{8,10},{9,11},{10,... | collective-permute-start | bytes 786440 | tf_op jit(solution)/shard_map/ppermute | solution.py:61
  15.8 18.9 %copy-start.1 = (bf16[256,1024]{1,0:T(8,128)(2,1)}, bf16[256,1024]{1,0:T(8,128)(2,1)S(1)}, u32[]{:S(2)}) copy-start(bf16[256,1024]{1,0:T(8,128)(2,1)S(1)} %constant_dynamic-update-slice_fusion.refs_0_) | copy-start | bytes 1572868
  15.8 19.0 %collective-permute-start.2 = (bf16[256,1024]{1,0:T(8,128)(2,1)S(1)}, bf16[256,1024]{1,0:T(8,128)(2,1)}, u32[]{:S(2)}, u32[]{:S(2)}) collective-permute-start(bf16[256,1024]{1,0:T(8,128)(2,1)S(1)} %constant_dynamic-update-slice_fusion.refs_0_), channel_id=1, source_target_pairs={{0,32},{1,97},{2,34},{3,99},{4,36},{5,101},{6,38},{7,103},{8,40},{... | collective-permute-start | bytes 1572872 | tf_op jit(solution)/shard_map/ppermute | solution.py:61
  23.5 11.3 %collective-permute-start.3 = (bf16[256,1024]{1,0:T(8,128)(2,1)S(1)}, bf16[256,1024]{1,0:T(8,128)(2,1)}, u32[]{:S(2)}, u32[]{:S(2)}) collective-permute-start(bf16[256,1024]{1,0:T(8,128)(2,1)S(1)} %constant_dynamic-update-slice_fusion.refs_0_), channel_id=1, source_target_pairs={{0,96},{1,33},{2,98},{3,35},{4,100},{5,37},{6,102},{7,39},{8,104},... | collective-permute-start | bytes 1572872 | tf_op jit(solution)/shard_map/ppermute | solution.py:61
  23.5 5.9 %collective-permute-start.7 = (bf16[128,1024]{1,0:T(8,128)(2,1)S(1)}, bf16[128,1024]{1,0:T(8,128)(2,1)S(1)}, u32[]{:S(2)}, u32[]{:S(2)}) collective-permute-start(bf16[128,1024]{1,0:T(8,128)(2,1)S(1)} %collective-permute-done.6), channel_id=1, source_target_pairs={{0,4},{1,13},{2,6},{3,15},{4,8},{5,1},{6,10},{7,3},{8,12},{9,5},{1... | collective-permute-start | bytes 786440 | tf_op jit(solution)/shard_map/ppermute | solution.py:61
  24.5 9.3 %collective-permute-start.8 = (bf16[128,1024]{1,0:T(8,128)(2,1)S(1)}, bf16[128,1024]{1,0:T(8,128)(2,1)}, u32[]{:S(2)}, u32[]{:S(2)}) collective-permute-start(bf16[128,1024]{1,0:T(8,128)(2,1)S(1)} %collective-permute-done.6), channel_id=1, source_target_pairs={{0,12},{1,5},{2,14},{3,7},{4,0},{5,9},{6,2},{7,11},{8,4},{9,13},{1... | collective-permute-start | bytes 786440 | tf_op jit(solution)/shard_map/ppermute | solution.py:61
  25.3 9.5 %collective-permute-start.5 = (bf16[128,1024]{1,0:T(8,128)(2,1)S(1)}, bf16[128,1024]{1,0:T(8,128)(2,1)S(1)}, u32[]{:S(2)}, u32[]{:S(2)}) collective-permute-start(bf16[128,1024]{1,0:T(8,128)(2,1)S(1)} %collective-permute-done.4), channel_id=1, source_target_pairs={{0,4},{1,13},{2,6},{3,15},{4,8},{5,1},{6,10},{7,3},{8,12},{9,5},{1... | collective-permute-start | bytes 786440 | tf_op jit(solution)/shard_map/ppermute | solution.py:61
  29.5 5.3 %copy-start.3 = (bf16[128,1024]{1,0:T(8,128)(2,1)}, bf16[128,1024]{1,0:T(8,128)(2,1)S(1)}, u32[]{:S(2)}) copy-start(bf16[128,1024]{1,0:T(8,128)(2,1)S(1)} %collective-permute-done.7) | copy-start | bytes 786436
  34.9 6.6 %collective-permute-start.10 = (bf16[512,1024]{1,0:T(8,128)(2,1)S(1)}, bf16[512,1024]{1,0:T(8,128)(2,1)S(1)}, u32[]{:S(2)}, u32[]{:S(2)}) collective-permute-start(bf16[512,1024]{1,0:T(8,128)(2,1)S(1)} %constant_dynamic-update-slice_fusion.2.rows), channel_id=1, source_target_pairs={{0,1},{1,0},{2,3},{3,2},{4,5},{5,4},{6,7},{7,6},{8,9},{9,8},{10,11... | collective-permute-start | bytes 3145736 | tf_op jit(solution)/shard_map/ppermute | solution.py:61
  37.4 17.2 %collective-permute-start.14 = (bf16[384,1024]{1,0:T(8,128)(2,1)S(1)}, bf16[384,1024]{1,0:T(8,128)(2,1)}, u32[]{:S(2)}, u32[]{:S(2)}) collective-permute-start(bf16[384,1024]{1,0:T(8,128)(2,1)S(1)} %pad_maximum_fusion.rows3), channel_id=1, source_target_pairs={{0,1},{1,0},{2,3},{3,2},{4,5},{5,4},{6,7},{7,6},{8,9},{9,8},{10,11... | collective-permute-start | bytes 2359304 | tf_op jit(solution)/shard_map/ppermute | solution.py:61
  37.5 10.9 %collective-permute-start.13 = (bf16[256,1024]{1,0:T(8,128)(2,1)}, bf16[256,1024]{1,0:T(8,128)(2,1)}, u32[]{:S(2)}, u32[]{:S(2)}) collective-permute-start(bf16[256,1024]{1,0:T(8,128)(2,1)} %collective-permute-done.2.refs_0_), channel_id=1, source_target_pairs={{0,32},{1,97},{2,34},{3,99},{4,36},{5,101},{6,38},{7,103},{8,40},{... | collective-permute-start | bytes 1572872 | tf_op jit(solution)/shard_map/ppermute | solution.py:61
  39.3 8.8 %collective-permute-start.11 = (bf16[128,1024]{1,0:T(8,128)(2,1)}, bf16[128,1024]{1,0:T(8,128)(2,1)S(1)}, u32[]{:S(2)}, u32[]{:S(2)}) collective-permute-start(bf16[128,1024]{1,0:T(8,128)(2,1)} %copy-done.3), channel_id=1, source_target_pairs={{0,4},{1,13},{2,6},{3,15},{4,8},{5,1},{6,10},{7,3},{8,12},{9,5},{1... | collective-permute-start | bytes 786440 | tf_op jit(solution)/shard_map/ppermute | solution.py:61
  40.6 7.7 %collective-permute-start.12 = (bf16[128,1024]{1,0:T(8,128)(2,1)}, bf16[128,1024]{1,0:T(8,128)(2,1)S(1)}, u32[]{:S(2)}, u32[]{:S(2)}) collective-permute-start(bf16[128,1024]{1,0:T(8,128)(2,1)} %copy-done.3), channel_id=1, source_target_pairs={{0,5},{1,12},{2,7},{3,14},{4,9},{5,0},{6,11},{7,2},{8,13},{9,4},{1... | collective-permute-start | bytes 786440 | tf_op jit(solution)/shard_map/ppermute | solution.py:61
  48.3 6.3 %copy-start = (bf16[512,1024]{1,0:T(8,128)(2,1)S(1)}, bf16[512,1024]{1,0:T(8,128)(2,1)}, u32[]{:S(2)}) copy-start(bf16[512,1024]{1,0:T(8,128)(2,1)} %get-tuple-element.32.b0) | copy-start | bytes 3145732
